TPU v7x, 32 devices: a whole 2x2x4 slice. The times are simulated.
32 devices in a mesh: gx: 4 (over z), gy: 8 (over y, x, core).
Axes of the slice: x: 2, y: 2, z: 4, core: 2. Of those that a mesh axis runs over, the one named last changes fastest.
Arguments:
- gaseous_rho: float32 [16, 768, 512], P(None, 'gy', 'gx'), may hold values from 0.5 to 2
- gaseous_flow_vector: float32 [3, 16, 768, 512], P(None, None, 'gy', 'gx'), may hold values from -1 to 1
- gaseous_kelvin: float32 [16, 768, 512], P(None, 'gy', 'gx'), may hold values from 0.5 to 2
- sender_tile_map: int32 [32, 256], P(('gx', 'gy')), may hold values from -1 to 1535, as said below
- receiver_arrival_rank: int32 [2048], P(('gx', 'gy')), may hold values from -1 to 255, as said below
- bin_active_number: int32 [2048], P(('gx', 'gy')), may hold values from 0 to 512, as said below
- grain_inertia: float32 [2048, 512], P(('gx', 'gy')), may hold values from 0.05 to 0.5
- grain_motion_vector: float32 [3, 2048, 512], P(None, ('gx', 'gy')), may hold values from -5 to 5
- grain_kelvin: float32 [2048, 512], P(('gx', 'gy')), may hold values from 0.5 to 4
- grain_voxel_number: int32 [2048, 512], P(('gx', 'gy')), may hold values from 0 to 127
- grain_substance_label: int32 [2048, 512], P(('gx', 'gy')), may hold values from 0 to 1
- exchange_factor: float32 [2, 2], replicated, may hold values from 0.5 to 4
Outputs:
- gas_state_out: float32 [5, 16, 768, 512], P(None, None, 'gy', 'gx')
- solid_state: float32 [4, 2048, 2, 128], P(None, ('gx', 'gy'))
Inputs may be any that keep to these rules, and one draw needn't show every extreme that they name: sender_tile_map[s, o * 8 + r] is the local block that device s sends as its r-th block to owner o, -1 where it sends fewer; the blocks of one device are distinct; only 8 devices send, each to every owner. `receiver_arrival_rank`: an owner's live slots come first, 48 or more of them, and name each sent block of that owner once; in each draw some owner has all 64 live and receives exactly 8 blocks from each sending device. `bin_active_number`: 0 exactly on slots with receiver_arrival_rank -1, else 512 // 2 or more; some slot holds 512.
All inputs are finite; a program needn't handle non-finite values.
Results may differ from a plain program's by a relative error of at most 0.0003.
Values sent between devices are 32-bit elements; how exact they have to be, the bound alone decides.
A program may use at most 128 MiB of HBM per device.

v0:
```python
import jax
import jax.numpy as jnp
from jax import lax
from jax.sharding import PartitionSpec as P

step_ratio = 0.08
group_size = 16


def extended(array, sides, width):
    for axis, dim in sides:
        count, length = (lax.axis_size(axis), array.shape[dim])
        up = [(i, (i + 1) % count) for i in range(count - 1)]
        down = [(j, i) for i, j in up]
        last = lax.slice_in_dim(array, length - width, length, axis=dim)
        leading = lax.slice_in_dim(array, 0, width, axis=dim)
        before = lax.ppermute(last, axis, up)
        after = lax.ppermute(leading, axis, down)
        array = jnp.concatenate([before, array, after], axis=dim)
    return array


def edge_mask(length):
    positions = jnp.arange(length + 1)
    return (positions == 0) | (positions == length)


def face_pair(quantity_array, direction):
    ndims = quantity_array.ndim
    lower_index = [slice(None)] * (ndims - 3) + [slice(1, -1)] * 3
    upper_index = list(lower_index)
    lower_index[ndims - 3 + direction] = slice(0, -1)
    upper_index[ndims - 3 + direction] = slice(1, None)
    return (quantity_array[tuple(lower_index)], quantity_array[tuple(upper_index)])


def advance(padded, wall_masks):
    density = padded[0]
    pressure = padded[0] * padded[4]
    conserved = jnp.concatenate(
        [padded[0:1], padded[0:1] * padded[1:4], padded[0:1] * padded[4:5]], 0
    )
    change = 0.0
    for direction in range(3):
        dens_lower, dens_upper = face_pair(density, direction)
        press_lower, press_upper = face_pair(pressure, direction)
        normal_lower, normal_upper = face_pair(padded[3 - direction], direction)
        face_speed = 0.5 * (normal_lower + normal_upper) - step_ratio * (
            press_upper - press_lower
        ) * 2.0 / (dens_lower + dens_upper)
        mask_shape = [1, 1, 1]
        mask_shape[direction] = -1
        face_speed = jnp.where(wall_masks[direction].reshape(mask_shape), 0.0, face_speed)
        cons_lower, cons_upper = face_pair(conserved, direction)
        face_flux = face_speed * jnp.where(face_speed > 0, cons_lower, cons_upper)
        count_faces = face_flux.shape[1 + direction]
        change = (
            change
            + lax.slice_in_dim(face_flux, 1, count_faces, axis=1 + direction)
            - lax.slice_in_dim(face_flux, 0, count_faces - 1, axis=1 + direction)
        )
    central = conserved[:, 1:-1, 1:-1, 1:-1]
    updated = central - step_ratio * change
    return jnp.concatenate(
        [updated[0:1], updated[1:4] / updated[0:1], updated[4:5] / updated[0:1]], 0
    )


def grain_quantities(grain_inertia, grain_motion_vector, grain_kelvin, bin_active_number):
    padding = grain_inertia.shape[1]
    present = jnp.arange(padding)[None, :] < bin_active_number[:, None]
    inertia_scaled = jnp.where(present, grain_inertia, 0.0)
    return jnp.stack(
        [
            inertia_scaled,
            inertia_scaled * grain_motion_vector[0],
            inertia_scaled * grain_motion_vector[1],
            inertia_scaled * grain_motion_vector[2],
            inertia_scaled * grain_kelvin,
        ],
        0,
    )


def couple(gas, grid, exchange_factor):
    gaseous_inertia = gas[0]
    gaseous_motion = gas[1:4]
    gaseous_enthalpy = gas[4]
    rigid_inertia = grid[0]
    solid_momentum = grid[1:4]
    rigid_enthalpy = grid[4]
    drag = exchange_factor[:, 0][None, :, None]
    thermal_coupler = exchange_factor[:, 1][None, :, None]
    drag_total = rigid_inertia + drag
    next_flow_vector = (
        gaseous_inertia * gaseous_motion + jnp.sum(drag * solid_momentum / drag_total, axis=2)
    ) / (gaseous_inertia + jnp.sum(drag * rigid_inertia / drag_total, axis=1))
    rigid_motion_vector = (solid_momentum + drag * next_flow_vector[:, :, None, :]) / drag_total
    summed_enthalpy = rigid_inertia + thermal_coupler
    next_kelvin = (
        gaseous_inertia * gaseous_enthalpy
        + jnp.sum(thermal_coupler * rigid_enthalpy / summed_enthalpy, axis=1)
    ) / (gaseous_inertia + jnp.sum(thermal_coupler * rigid_inertia / summed_enthalpy, axis=1))
    rigid_kelvin = (rigid_enthalpy + thermal_coupler * next_kelvin[:, None, :]) / summed_enthalpy
    increment_changes = jnp.concatenate(
        [next_flow_vector - gaseous_motion, (next_kelvin - gaseous_enthalpy)[None]], 0
    )
    rigid_constituent = jnp.concatenate([rigid_motion_vector, rigid_kelvin[None]], 0)
    return (increment_changes, rigid_constituent)


def onehot_sums(quantity_array, target, width):
    slot_total, padding = target.shape
    groups = slot_total // group_size
    columns = jnp.arange(2 * width)

    def group_sum(pieces):
        group_values, group_target = pieces
        onehot_table = (group_target[..., None] == columns).astype(jnp.float32)
        return jnp.einsum(
            "fsp,spc->fsc", group_values, onehot_table, precision=lax.Precision.HIGHEST
        )

    summed = lax.map(
        group_sum,
        (
            quantity_array.reshape(5, groups, group_size, padding).transpose(1, 0, 2, 3),
            target.reshape(groups, group_size, padding),
        ),
    )
    return summed.transpose(1, 0, 2, 3).reshape(5, slot_total, 2, width)


def per_device(
    gaseous_rho,
    gaseous_flow_vector,
    gaseous_kelvin,
    sender_tile_map,
    receiver_arrival_rank,
    bin_active_number,
    grain_inertia,
    grain_motion_vector,
    grain_kelvin,
    grain_voxel_number,
    grain_substance_label,
    exchange_factor,
):
    depth, height, width = gaseous_rho.shape
    voxel_record = jnp.concatenate(
        [gaseous_rho[None], gaseous_flow_vector, gaseous_kelvin[None]], 0
    )
    haloed = extended(voxel_record, (("gx", 3), ("gy", 2)), 1)
    padded = jnp.pad(haloed, ((0, 0), (1, 1), (0, 0), (0, 0)))
    rows_global = lax.axis_index("gy") * height + jnp.arange(height + 1)
    rows_wall = (rows_global == 0) | (rows_global == height * lax.axis_size("gy"))
    cols_global = lax.axis_index("gx") * width + jnp.arange(width + 1)
    cols_wall = (cols_global == 0) | (cols_global == width * lax.axis_size("gx"))
    advanced = advance(padded, [edge_mask(depth), rows_wall, cols_wall])
    block_count = depth * height
    blocks = advanced.reshape(5, block_count, width)
    outgoing_index = sender_tile_map[0]
    devices = lax.axis_size("gx") * lax.axis_size("gy")
    capacity = outgoing_index.shape[0] // devices
    outgoing = blocks[:, jnp.maximum(outgoing_index, 0)]
    incoming = lax.all_to_all(
        outgoing.reshape(5, devices, capacity, width),
        ("gx", "gy"),
        split_axis=1,
        concat_axis=1,
        tiled=True,
    )
    incoming = incoming.reshape(5, devices * capacity, width)
    live_slot = receiver_arrival_rank >= 0
    gas = incoming[:, jnp.maximum(receiver_arrival_rank, 0)]
    quantity_array = grain_quantities(
        grain_inertia, grain_motion_vector, grain_kelvin, bin_active_number
    )
    target = grain_substance_label * width + grain_voxel_number
    grid = onehot_sums(quantity_array, target, width)
    increment_changes, rigid_constituent = couple(gas, grid, exchange_factor)
    solid_state = jnp.where(live_slot[None, :, None, None], rigid_constituent, 0.0)
    returning = (
        jnp.zeros((4, devices * capacity, width), jnp.float32)
        .at[:, jnp.where(live_slot, receiver_arrival_rank, devices * capacity)]
        .add(increment_changes, mode="drop")
    )
    returned = lax.all_to_all(
        returning.reshape(4, devices, capacity, width),
        ("gx", "gy"),
        split_axis=1,
        concat_axis=1,
        tiled=True,
    )
    returned = returned.reshape(4, devices * capacity, width)
    gains = (
        jnp.zeros((4, block_count, width), jnp.float32)
        .at[:, jnp.where(outgoing_index >= 0, outgoing_index, block_count)]
        .add(returned, mode="drop")
    )
    final = jnp.concatenate([blocks[0:1], blocks[1:5] + gains], 0).reshape(5, depth, height, width)
    return (final, solid_state)


def solution(mesh):
    placed = (
        P(None, "gy", "gx"),
        P(None, None, "gy", "gx"),
        P(None, "gy", "gx"),
        P(("gx", "gy"), None),
        P(("gx", "gy")),
        P(("gx", "gy")),
        P(("gx", "gy"), None),
        P(None, ("gx", "gy"), None),
        P(("gx", "gy"), None),
        P(("gx", "gy"), None),
        P(("gx", "gy"), None),
        P(),
    )
    return jax.shard_map(
        per_device,
        mesh=mesh,
        in_specs=placed,
        out_specs=(P(None, None, "gy", "gx"), P(None, ("gx", "gy"), None, None)),
        check_vma=False,
    )
```

profile of v0, /device:TPU:0, one launch (start us, length us, event | category | flops | bytes accessed | tf_op | source)
XLA Modules:
  0.0 243.2 jit_solution(4419879217947361820)
XLA Ops:
  9.6 5.5 %collective-permute-start = (f32[5,16,96,1]{2,1,3,0:T(8,128)}, f32[5,16,96,1]{2,1,3,0:T(8,128)}, u32[]{:S(2)}, u32[]{:S(2)}) collective-permute-start(f32[5,16,96,1]{2,1,3,0:T(8,128)} %get-tuple-element.74), channel_id=1, source_target_pairs={{0,8},{8,16},{16,24},{1,9},{9,17},{17,25},{2,10},{10,18},{18,26},{... | collective-permute-start | bytes 92168 | tf_op jit(solution)/shard_map/ppermute | solution.py:17
  28.9 17.4 %while.11 = (s32[]{:T(128)}, f32[4,5,16,256]{3,1,2,0:T(8,128)}, s32[4,16,512]{2,1,0:T(8,128)S(1)}, f32[4,5,16,512]{3,1,2,0:T(8,128)}, s32[]{:T(128)}) while((s32[]{:T(128)}, f32[4,5,16,256]{3,1,2,0:T(8,128)}, s32[4,16,512]{2,1,0:T(8,128)S(1)}, f32[4,5,16,512]{3,1,2,0:T(8,128)}, s32[]{:T(128)}) %tuple.54), condition=%wide.region_1.2_spmd.clone, body=%wide.region_0.1_spmd.clone.sunk | while | flops 127926272 | bytes 492609 | solution.py:124
  28.9 4.4 %fusion.51 = f32[4,5,16,256]{3,1,2,0:T(8,128)} fusion(f32[4,5,16,256]{3,1,2,0:T(8,128)} %get-tuple-element.121, s32[]{:T(128)} %get-tuple-element.120, s32[16,512]{1,0:T(8,128)S(1)} %dynamic-slice_bitcast_fusion.2, f32[4,5,16,512]{3,1,2,0:T(8,128)} %get-tuple-element.128), kind=kOutput, calls=%fused_computation.9.clone.1 | convolution fusion | flops 127926272 | bytes 427008 | tf_op jit(solution)/shard_map/while/body/eval_jaxpr/fsp,spc->fsc/dot_general | solution.py:120
  33.2 4.4 %fusion.51 = f32[4,5,16,256]{3,1,2,0:T(8,128)} fusion(f32[4,5,16,256]{3,1,2,0:T(8,128)} %get-tuple-element.121, s32[]{:T(128)} %get-tuple-element.120, s32[16,512]{1,0:T(8,128)S(1)} %dynamic-slice_bitcast_fusion.2, f32[4,5,16,512]{3,1,2,0:T(8,128)} %get-tuple-element.128), kind=kOutput, calls=%fused_computation.9.clone.1 | convolution fusion | flops 127926272 | bytes 427008 | tf_op jit(solution)/shard_map/while/body/eval_jaxpr/fsp,spc->fsc/dot_general | solution.py:120
  37.6 4.4 %fusion.51 = f32[4,5,16,256]{3,1,2,0:T(8,128)} fusion(f32[4,5,16,256]{3,1,2,0:T(8,128)} %get-tuple-element.121, s32[]{:T(128)} %get-tuple-element.120, s32[16,512]{1,0:T(8,128)S(1)} %dynamic-slice_bitcast_fusion.2, f32[4,5,16,512]{3,1,2,0:T(8,128)} %get-tuple-element.128), kind=kOutput, calls=%fused_computation.9.clone.1 | convolution fusion | flops 127926272 | bytes 427008 | tf_op jit(solution)/shard_map/while/body/eval_jaxpr/fsp,spc->fsc/dot_general | solution.py:120
  41.9 4.3 %fusion.51 = f32[4,5,16,256]{3,1,2,0:T(8,128)} fusion(f32[4,5,16,256]{3,1,2,0:T(8,128)} %get-tuple-element.121, s32[]{:T(128)} %get-tuple-element.120, s32[16,512]{1,0:T(8,128)S(1)} %dynamic-slice_bitcast_fusion.2, f32[4,5,16,512]{3,1,2,0:T(8,128)} %get-tuple-element.128), kind=kOutput, calls=%fused_computation.9.clone.1 | convolution fusion | flops 127926272 | bytes 427008 | tf_op jit(solution)/shard_map/while/body/eval_jaxpr/fsp,spc->fsc/dot_general | solution.py:120
  48.2 5.8 %fusion.44 = (f32[5,16,1,130]{2,1,3,0:T(8,128)}, f32[5,16,1,130]{2,1,3,0:T(8,128)}) fusion(f32[5,16,96,130]{2,1,3,0:T(8,128)S(1)} %pad_maximum_fusion.1), kind=kLoop, calls=%fused_computation.124 | loop fusion | bytes 166400 | tf_op jit(solution)/shard_map/slice | solution.py:15
  54.0 4.9 %copy.47 = f32[5,16,1,130]{3,1,2,0:T(8,128)S(1)} copy(f32[5,16,1,130]{2,1,3,0:T(8,128)} %get-tuple-element.69) | data formatting | bytes 83200 | tf_op jit(solution)/shard_map/slice | solution.py:15
  60.3 5.5 %copy.48 = f32[5,16,1,130]{3,1,2,0:T(8,128)} copy(f32[5,16,1,130]{2,1,3,0:T(8,128)} %get-tuple-element.70) | data formatting | bytes 83200 | tf_op jit(solution)/shard_map/slice | solution.py:16
  70.1 4.7 %copy.49 = f32[5,16,1,130]{2,1,3,0:T(8,128)} copy(f32[5,16,1,130]{3,1,2,0:T(8,128)S(1)} %collective-permute-done.2) | data formatting | bytes 83200 | tf_op jit(solution)/shard_map/ppermute | solution.py:17
  74.8 5.4 %copy.50 = f32[5,16,1,130]{2,1,3,0:T(8,128)} copy(f32[5,16,1,130]{3,1,2,0:T(8,128)} %collective-permute-done.3) | data formatting | bytes 83200 | tf_op jit(solution)/shard_map/ppermute | solution.py:18
  80.2 10.1 %select_maximum_fusion = f32[5,18,98,130]{2,1,3,0:T(8,128)S(1)} fusion(f32[5,16,1,130]{2,1,3,0:T(8,128)} %copy.50, f32[5,16,1,130]{2,1,3,0:T(8,128)} %copy.49, f32[5,16,96,1]{2,1,3,0:T(8,128)} %collective-permute-done.1, f32[5,16,96,1]{2,1,3,0:T(8,128)} %collective-permute-done, f32[1,16,96,128]{2,1,3,0:T(8,128)} %bitcast.91, ...), kind=kLoop, calls=%fused_computation.16 | loop fusion | flops 18345600 | bytes 8663200 | tf_op jit(solution)/shard_map/concatenate | solution.py:19
  99.3 6.2 %fusion.10 = f32[5,17,96,128]{2,1,3,0:T(8,128)} fusion(f32[5,18,98,130]{2,1,3,0:T(8,128)S(1)} %pad_maximum_fusion, f32[17,96,128]{1,0,2:T(8,128)S(1)} %get-tuple-element.58, pred[17,96,128]{1,0,2:T(8,128)(4,1)S(1)} %get-tuple-element.57), kind=kLoop, calls=%fused_computation.25 | loop fusion | flops 2088960 | bytes 13578240 | tf_op jit(solution)/shard_map/mul | solution.py:55
  105.5 5.1 %fusion.14 = f32[5,16,97,128]{2,1,3,0:T(8,128)} fusion(f32[5,18,98,130]{2,1,3,0:T(8,128)S(1)} %pad_maximum_fusion, f32[16,97,128]{1,0,2:T(8,128)} %get-tuple-element.60, pred[16,97,128]{1,0,2:T(8,128)(4,1)} %get-tuple-element.59), kind=kLoop, calls=%fused_computation.36 | loop fusion | flops 1986560 | bytes 12912640 | tf_op jit(solution)/shard_map/mul | solution.py:55
  110.6 6.0 %broadcast_compare_fusion.1 = (pred[16,96,129]{1,0,2:T(8,128)(4,1)}, f32[16,96,129]{1,0,2:T(8,128)}) fusion(f32[18,98,130]{1,0,2:T(8,128)S(1)} %get-tuple-element.64, f32[18,98,130]{1,0,2:T(8,128)} %copy-done, f32[18,98,130]{1,0,2:T(8,128)} %get-tuple-element.68, pred[129]{0:T(512)(128)(4,1)S(1)} %compare_or_fusion), kind=kLoop, calls=%fused_computation.74 | loop fusion | flops 1783296 | bytes 5746305 | tf_op jit(solution)/shard_map/gt | solution.py:55
  116.6 6.4 %fusion.11 = f32[5,16,96,129]{2,1,3,0:T(8,128)} fusion(f32[5,18,98,130]{2,1,3,0:T(8,128)S(1)} %pad_maximum_fusion, f32[16,96,129]{1,0,2:T(8,128)} %get-tuple-element.62, pred[16,96,129]{1,0,2:T(8,128)(4,1)} %get-tuple-element.61), kind=kLoop, calls=%fused_computation.28 | loop fusion | flops 1981440 | bytes 12879360 | tf_op jit(solution)/shard_map/mul | solution.py:55
  123.0 14.7 %fusion.13 = f32[5,16,96,128]{2,1,3,0:T(8,128)} fusion(f32[5,16,96,129]{2,1,3,0:T(8,128)} %fusion.11, f32[5,16,97,128]{2,1,3,0:T(8,128)} %fusion.14, f32[5,17,96,128]{2,1,3,0:T(8,128)} %fusion.10, f32[5,18,98,130]{2,1,3,0:T(8,128)S(1)} %pad_maximum_fusion), kind=kLoop, calls=%fused_computation.31 | loop fusion | flops 6881280 | bytes 31457280 | tf_op jit(solution)/shard_map/sub | solution.py:63
  144.7 5.7 %copy.52 = f32[5,16,96,128]{3,0,2,1:T(8,128)} copy(f32[5,16,96,128]{2,1,3,0:T(8,128)} %pad_maximum_fusion.2) | data formatting | bytes 7864320 | tf_op jit(solution)/shard_map/concatenate | solution.py:64
  150.5 4.5 %gather_fusion = f32[256,5,128]{2,1,0:T(8,128)} fusion(f32[5,1536,128]{2,0,1:T(8,128)} %bitcast.94, s32[1024]{0:T(1024)S(1)} %pad_clamp_fusion.1), kind=kCustom, calls=%fused_computation | custom fusion | bytes 1311744 | tf_op jit(solution)/shard_map/gather | solution.py:164
  157.2 10.1 %all-to-all-start = ((f32[5,32,8,128]{3,2,0,1:T(8,128)}), f32[5,32,8,128]{3,2,0,1:T(8,128)}, u32[]{:S(2)}, u32[]{:S(2)}) async-start(f32[5,32,8,128]{3,2,0,1:T(8,128)} %copy.53), calls=%async_computation | async-start | bytes 1310720 | tf_op jit(solution)/shard_map/all_to_all | solution.py:165
  171.4 13.5 %all-to-all-done = f32[5,32,8,128]{3,2,0,1:T(8,128)} async-done(((f32[5,32,8,128]{3,2,0,1:T(8,128)}), f32[5,32,8,128]{3,2,0,1:T(8,128)}, u32[]{:S(2)}, u32[]{:S(2)}) %all-to-all-start) | async-done | bytes 655392 | tf_op jit(solution)/shard_map/all_to_all | solution.py:165
  196.0 7.1 %scatter_fusion = f32[4,256,128]{2,0,1:T(4,128)} fusion(f32[4,256,128]{2,0,1:T(4,128)} %broadcast_in_dim.124, s32[64]{0:T(128)S(1)} %get-tuple-element.89, f32[64,4,128]{2,1,0:T(4,128)} %maximum_bitcast_fusion), kind=kCustom, calls=%fused_computation.2 | custom fusion | flops 32768 | bytes 393472 | tf_op jit(solution)/shard_map/scatter-add | solution.py:185
  203.1 3.6 %all-to-all-start.1 = ((f32[4,32,8,128]{3,0,2,1:T(4,128)}), f32[4,32,8,128]{3,0,2,1:T(4,128)}, u32[]{:S(2)}, u32[]{:S(2)}) async-start(f32[4,32,8,128]{3,0,2,1:T(4,128)} %bitcast.96), calls=%async_computation.1 | async-start | bytes 1048576 | tf_op jit(solution)/shard_map/all_to_all | solution.py:187
  222.3 17.6 %scatter_fusion.1 = f32[4,1536,128]{2,0,1:T(4,128)S(1)} fusion(f32[4,1536,128]{2,0,1:T(4,128)S(1)} %bitcast.92, s32[256]{0:T(256)S(1)} %bitcast.116, f32[256,4,128]{2,1,0:T(4,128)} %bitcast.35), kind=kCustom, calls=%fused_computation.3 | custom fusion | flops 131072 | bytes 1573888 | tf_op jit(solution)/shard_map/scatter-add | solution.py:198
  (97 shorter events, 82.3 us)
Async XLA Ops:
  3.1 13.3 %copy-start.11 = (s32[1,256]{1,0:T(1,128)S(1)}, s32[1,256]{1,0:T(1,128)}, u32[]{:S(2)}) copy-start(s32[1,256]{1,0:T(1,128)} %param.17) | copy-start | bytes 3076
  3.1 13.3 %copy-start.9 = (f32[64,512]{1,0:T(8,128)S(1)}, f32[64,512]{1,0:T(8,128)}, u32[]{:S(2)}) copy-start(f32[64,512]{1,0:T(8,128)} %param.22) | copy-start | bytes 393220
  3.1 13.3 %copy-start.12 = (s32[64]{0:T(128)S(1)}, s32[64]{0:T(128)}, u32[]{:S(2)}) copy-start(s32[64]{0:T(128)} %param.19) | copy-start | bytes 772
  9.6 36.7 %collective-permute-start = (f32[5,16,96,1]{2,1,3,0:T(8,128)}, f32[5,16,96,1]{2,1,3,0:T(8,128)}, u32[]{:S(2)}, u32[]{:S(2)}) collective-permute-start(f32[5,16,96,1]{2,1,3,0:T(8,128)} %get-tuple-element.74), channel_id=1, source_target_pairs={{0,8},{8,16},{16,24},{1,9},{9,17},{17,25},{2,10},{10,18},{18,26},{... | collective-permute-start | bytes 92168 | tf_op jit(solution)/shard_map/ppermute | solution.py:17
  15.1 31.2 %collective-permute-start.1 = (f32[5,16,96,1]{2,1,3,0:T(8,128)}, f32[5,16,96,1]{2,1,3,0:T(8,128)}, u32[]{:S(2)}, u32[]{:S(2)}) collective-permute-start(f32[5,16,96,1]{2,1,3,0:T(8,128)} %get-tuple-element.75), channel_id=1, source_target_pairs={{8,0},{16,8},{24,16},{9,1},{17,9},{25,17},{10,2},{18,10},{26,18},{... | collective-permute-start | bytes 92168 | tf_op jit(solution)/shard_map/ppermute | solution.py:18
  58.9 11.2 %collective-permute-start.2 = (f32[5,16,1,130]{3,1,2,0:T(8,128)S(1)}, f32[5,16,1,130]{3,1,2,0:T(8,128)S(1)}, u32[]{:S(2)}, u32[]{:S(2)}) collective-permute-start(f32[5,16,1,130]{3,1,2,0:T(8,128)S(1)} %copy.47), channel_id=1, source_target_pairs={{0,1},{1,2},{2,3},{3,4},{4,5},{5,6},{6,7},{8,9},{9,10},{10,11},{11... | collective-permute-start | bytes 124808 | tf_op jit(solution)/shard_map/ppermute | solution.py:17
  65.8 9.0 %collective-permute-start.3 = (f32[5,16,1,130]{3,1,2,0:T(8,128)}, f32[5,16,1,130]{3,1,2,0:T(8,128)}, u32[]{:S(2)}, u32[]{:S(2)}) collective-permute-start(f32[5,16,1,130]{3,1,2,0:T(8,128)} %copy.48), channel_id=1, source_target_pairs={{1,0},{2,1},{3,2},{4,3},{5,4},{6,5},{7,6},{9,8},{10,9},{11,10},{12... | collective-permute-start | bytes 124808 | tf_op jit(solution)/shard_map/ppermute | solution.py:18
  93.0 3.0 %copy-start = (f32[18,98,130]{1,0,2:T(8,128)}, f32[18,98,130]{1,0,2:T(8,128)S(1)}, u32[]{:S(2)}) copy-start(f32[18,98,130]{1,0,2:T(8,128)S(1)} %bitcast_multiply_fusion) | copy-start | bytes 2751844
  96.0 2.7 %copy-start.4 = (f32[1,18,98,130]{2,1,3,0:T(8,128)S(1)}, f32[1,18,98,130]{2,1,3,0:T(8,128)}, u32[]{:S(2)}) copy-start(f32[1,18,98,130]{2,1,3,0:T(8,128)} %get-tuple-element.66) | copy-start | bytes 2751844
  96.0 2.7 %copy-start.5 = (f32[1,18,98,130]{2,1,3,0:T(8,128)S(1)}, f32[1,18,98,130]{2,1,3,0:T(8,128)}, u32[]{:S(2)}) copy-start(f32[1,18,98,130]{2,1,3,0:T(8,128)} %get-tuple-element.67) | copy-start | bytes 2751844
  137.7 3.7 %copy-start.1 = (f32[5,16,96,128]{2,1,3,0:T(8,128)S(1)}, f32[5,16,96,128]{2,1,3,0:T(8,128)}, u32[]{:S(2)}) copy-start(f32[5,16,96,128]{2,1,3,0:T(8,128)} %fusion.13) | copy-start | bytes 11796484
  139.7 2.0 copy-start.2
  139.7 2.0 copy-start.3
  144.7 22.6 %copy-start.13 = (s32[64]{0:T(128)S(1)}, s32[64]{0:T(128)}, u32[]{:S(2)}) copy-start(s32[64]{0:T(128)} %param.18) | copy-start | bytes 772
  144.7 22.6 %copy-start.10 = (f32[2,2]{1,0:T(2,128)S(1)}, f32[2,2]{1,0:T(2,128)}, u32[]{:S(2)}) copy-start(f32[2,2]{1,0:T(2,128)} %param.25) | copy-start | bytes 52
  157.2 27.7 %all-to-all-start = ((f32[5,32,8,128]{3,2,0,1:T(8,128)}), f32[5,32,8,128]{3,2,0,1:T(8,128)}, u32[]{:S(2)}, u32[]{:S(2)}) async-start(f32[5,32,8,128]{3,2,0,1:T(8,128)} %copy.53), calls=%async_computation | async-start | bytes 1310720 | tf_op jit(solution)/shard_map/all_to_all | solution.py:165
  169.8 0.6 copy-start.7
  190.8 1.8 copy-start.8
  203.1 19.2 %all-to-all-start.1 = ((f32[4,32,8,128]{3,0,2,1:T(4,128)}), f32[4,32,8,128]{3,0,2,1:T(4,128)}, u32[]{:S(2)}, u32[]{:S(2)}) async-start(f32[4,32,8,128]{3,0,2,1:T(4,128)} %bitcast.96), calls=%async_computation.1 | async-start | bytes 1048576 | tf_op jit(solution)/shard_map/all_to_all | solution.py:187
  239.9 1.1 copy-start.6
where the time goes:
time: 246 us; the launch traced here: 243 us
  other arithmetic  109 us (44%)
  local copies, waits for them, and re-layouts  76 us (31%)
  starting transfers between devices  23.3 us (9%)
  matrix products  17.4 us (7%)
  waiting for transfers between devices  16.2 us (7%)
    mul x3, other arithmetic, advance(): face_flux = face_speed * jnp.where(face_speed > 0, cons_lower, cons_upper)  17.7 us
    scatter-add x1, other arithmetic, per_device(): gains = jnp.zeros((4, block_count, width), jnp.float32).at[:, jnp.where(o...  17.6 us
    dot_general x4, matrix products, group_sum(): jnp.einsum('fsp,spc->fsc', group_values, onehot_table, precision=lax.Prec...  17.4 us
    sub x1, other arithmetic, advance(): updated = central - step_ratio * change  14.7 us
    all_to_all x1, waiting for transfers between devices, per_device(): lax.all_to_all(outgoing.reshape(5, devices, capacity, width), ('gx', 'gy'...  13.5 us
    concatenate x2, other arithmetic, extended(): array = jnp.concatenate([before, array, after], axis=dim)  12 us
    gt x3, other arithmetic, advance(): face_flux = face_speed * jnp.where(face_speed > 0, cons_lower, cons_upper)  11.2 us
    slice x2, local copies, waits for them, and re-layouts, extended(): last = lax.slice_in_dim(array, length - width, length, axis=dim)  10.7 us
  transfers between devices with their start and end apart: 6, of which 2 were waited for; matrix products, arithmetic and copies ran while one was open for 24% of the time, Pallas kernels for 0%

commit v1 on v0

v1 whole, which is shorter than its diff:
```python
import functools

import jax
import jax.numpy as jnp
from jax import lax
from jax.experimental import pallas as pl
from jax.experimental.pallas import tpu as pltpu
from jax.sharding import PartitionSpec as P

MESH = pl.DeviceIdType.MESH
VMEM = pl.BlockSpec(memory_space=pltpu.VMEM)
SMEM = pl.BlockSpec(memory_space=pltpu.SMEM)
step_ratio = 0.08
limit = 56 * 1024 * 1024
sent = 6
back = 4


def coefficients(ex_ref, m):
    rows = lax.broadcasted_iota(jnp.int32, (8, 128), 0)
    return jnp.where(rows < 4, ex_ref[m, 0], ex_ref[m, 1])


def bin_kernel(
    cap, rank_ref, count_ref, ex_ref, mass_ref, vel_ref, temp_ref, vox_ref, lab_ref, pay_ref, sums_ref
):
    slots, padding = mass_ref.shape
    width = pay_ref.shape[2]
    pay_ref[...] = jnp.zeros_like(pay_ref)
    rows = lax.broadcasted_iota(jnp.int32, (8, padding), 0)
    lane = lax.broadcasted_iota(jnp.int32, (1, padding), 1)
    cells = lax.broadcasted_iota(jnp.int32, (width, padding), 0)
    factor = [coefficients(ex_ref, m) for m in range(2)]
    unroll = 4

    def body(i, carry):
        for u in range(unroll):
            k = i * unroll + u
            here = pl.ds(k, 1)
            mass = jnp.where(lane < count_ref[k], mass_ref[here, :], 0.0)
            base = jnp.where(rows == 4, temp_ref[here, :], 1.0)
            for c in range(3):
                base = jnp.where(rows == c + 1, vel_ref[c, here, :], base)
            base = base * mass
            label = lab_ref[here, :]
            values = jnp.concatenate(
                [jnp.where(label == 0, base, 0.0), jnp.where(label == 1, base, 0.0)], 0
            )
            high = values.astype(jnp.bfloat16)
            low = (values - high.astype(jnp.float32)).astype(jnp.bfloat16)
            onehot = jnp.where(cells == vox_ref[here, :], 1.0, 0.0).astype(jnp.bfloat16)
            total = lax.dot_general(
                jnp.concatenate([high, low], 0),
                onehot,
                (((1,), (1,)), ((), ())),
                preferred_element_type=jnp.float32,
            )
            total = total[:16] + total[16:]
            sums_ref[k] = total
            pay = 0.0
            for m in range(2):
                part = total[8 * m : 8 * m + 8]
                pay = pay + factor[m] * part / (part[0:1] + factor[m])
            v = rank_ref[k]

            @pl.when(v >= 0)
            def _():
                s = v // cap
                r = v % cap
                for j in range(sent):
                    pay_ref[s, pl.ds(j * cap + r, 1), :] = pay[j : j + 1]

        return carry

    lax.fori_loop(0, slots // unroll, body, 0)


def face(a, b, ua, ub, wall):
    speed = 0.5 * (ua + ub) - (2.0 * step_ratio) * (b[4] - a[4]) / (a[0] + b[0])
    speed = jnp.where(wall, 0.0, speed)
    ahead = speed > 0
    return [speed * jnp.where(ahead, x, y) for x, y in zip(a, b)]


def conserve(prim):
    rho = prim[0]
    return [rho] + [rho * q for q in prim[1:]]


def grid_kernel(
    n_gx,
    n_gy,
    map_ref,
    rho_ref,
    vel_ref,
    temp_ref,
    pay_ref,
    adv_ref,
    new_ref,
    ret_ref,
    xsend,
    xrecv,
    ysend,
    yrecv,
    got,
    home,
    ext,
    flux_z,
    picked,
    halo_send,
    halo_recv,
    pay_send,
    pay_recv,
    back_send,
    back_recv,
):
    n = n_gx * n_gy
    depth, height, width = rho_ref.shape
    cap = map_ref.shape[1] // n
    gx = lax.axis_index("gx")
    gy = lax.axis_index("gy")
    me = gx * n_gy + gy

    def place(d):
        return (d // n_gy, lax.rem(d, n_gy))

    barrier = pltpu.get_barrier_semaphore()

    def greet(k, carry):
        d = lax.rem(me + k, n)
        pl.semaphore_signal(barrier, inc=1, device_id=place(d), device_id_type=MESH)
        return carry

    lax.fori_loop(1, n, greet, 0)

    def prim(f, z, rows):
        if f == 0:
            return rho_ref[z, rows, :]
        if f == 4:
            return temp_ref[z, rows, :]
        return vel_ref[f - 1, z, rows, :]

    whole = pl.ds(0, height)
    lanes = lax.broadcasted_iota(jnp.int32, (height, width), 1)

    def pack(z, carry):
        low, high = carry
        for f in range(5):
            spot = f * depth + z
            x = prim(f, z, whole)
            ysend[0, f, pl.ds(z, 1), :] = x[0:1]
            ysend[1, f, pl.ds(z, 1), :] = x[height - 1 : height]
            low = jnp.where(lanes == spot, pltpu.roll(x, spot, 1), low)
            high = jnp.where(lanes == spot, pltpu.roll(x, spot + 1, 1), high)
        return (low, high)

    zero = jnp.zeros((height, width), jnp.float32)
    low, high = lax.fori_loop(0, depth, pack, (zero, zero))
    xsend[0] = low
    xsend[1] = high
    pl.semaphore_wait(barrier, n - 1)

    def halo(which, side, device):
        src, dst = ((xsend, xrecv), (ysend, yrecv))[which]
        return pltpu.make_async_remote_copy(
            src_ref=src.at[side],
            dst_ref=dst.at[1 - side],
            send_sem=halo_send.at[2 * which + side],
            recv_sem=halo_recv.at[2 * which + 1 - side],
            device_id=device,
            device_id_type=MESH,
        )

    sides = (
        (0, 0, gx > 0, (gx - 1, gy)),
        (0, 1, gx < n_gx - 1, (gx + 1, gy)),
        (1, 0, gy > 0, (gx, gy - 1)),
        (1, 1, gy < n_gy - 1, (gx, gy + 1)),
    )
    for which, side, there, device in sides:

        @pl.when(there)
        def _(which=which, side=side, device=device):
            halo(which, side, device).start()

    def outward(k):
        d = lax.rem(me + k, n)
        return pltpu.make_async_remote_copy(
            src_ref=pay_ref.at[d],
            dst_ref=got.at[me],
            send_sem=pay_send.at[k],
            recv_sem=pay_recv.at[k],
            device_id=place(d),
            device_id_type=MESH,
        )

    def send_out(k, carry):
        outward(k).start()
        return carry

    lax.fori_loop(1, n, send_out, 0)

    for which, side, there, device in sides:
        recv = (xrecv, yrecv)[which]

        @pl.when(there)
        def _(which=which, side=side, device=device):
            pltpu.make_async_remote_copy(
                src_ref=(xsend, ysend)[which].at[side],
                dst_ref=(xrecv, yrecv)[which].at[side],
                send_sem=halo_send.at[2 * which + side],
                recv_sem=halo_recv.at[2 * which + side],
                device_id=device,
                device_id_type=MESH,
            ).wait()

        @pl.when(jnp.logical_not(there))
        def _(recv=recv, side=side):
            recv[side] = jnp.ones(recv.shape[1:], jnp.float32)

    west, east = gx == 0, gx == n_gx - 1
    south, north = gy == 0, gy == n_gy - 1
    flux_z[...] = jnp.zeros_like(flux_z)
    ext[...] = jnp.ones_like(ext)
    chunk = 32 if height % 32 == 0 else height
    tile = (chunk, width)
    lane = lax.broadcasted_iota(jnp.int32, tile, 1)
    row = lax.broadcasted_iota(jnp.int32, (chunk + 8, width), 0)
    first, last = lane == 0, lane == width - 1
    wall_low = jnp.logical_and(first, west)
    wall_high = jnp.logical_and(last, east)

    def plane(z, carry):
        above = jnp.minimum(z + 1, depth - 1)
        at_top = z == depth - 1
        here = conserve([prim(f, z, whole) for f in range(5)])
        for f in range(5):
            ext[f, 8 : 8 + height, :] = here[f]
        ext[5, 8 : 8 + height, :] = prim(2, z, whole)
        for side, at in ((0, 7), (1, 8 + height)):
            edge = [yrecv[side, f, pl.ds(z, 1), :] for f in range(5)]
            for f, q in enumerate(conserve(edge)):
                ext[f, at : at + 1, :] = q
            ext[5, at : at + 1, :] = edge[2]
        for y0 in range(0, height, chunk):
            rows = pl.ds(y0, chunk)
            own = [prim(f, z, rows) for f in range(5)]
            cons = conserve(own)
            change = [0.0] * 5
            up = [prim(f, above, rows) for f in range(5)]
            flux = face(cons, conserve(up), own[3], up[3], at_top)
            for f in range(5):
                change[f] = flux[f] - flux_z[f, rows, :]
                flux_z[f, rows, :] = flux[f]
            lower = [ext[f, pl.ds(7 + y0, chunk + 8), :] for f in range(6)]
            upper = [ext[f, pl.ds(8 + y0, chunk + 8), :] for f in range(6)]
            wall = False
            if y0 == 0:
                wall = jnp.logical_and(row == 0, south)
            if y0 + chunk == height:
                wall = jnp.logical_or(wall, jnp.logical_and(row == chunk, north))
            flux = face(lower[:5], upper[:5], lower[5], upper[5], wall)
            for f in range(5):
                change[f] = change[f] + (flux[f][1 : chunk + 1] - flux[f][:chunk])
            left, right = [], []
            for f in range(5):
                spot = f * depth + z
                left.append(
                    jnp.where(
                        first,
                        pltpu.roll(xrecv[0, rows, :], lax.rem(width - spot, width), 1),
                        pltpu.roll(own[f], 1, 1),
                    )
                )
                right.append(
                    jnp.where(
                        last,
                        pltpu.roll(xrecv[1, rows, :], width - 1 - spot, 1),
                        pltpu.roll(own[f], width - 1, 1),
                    )
                )
            flux = face(conserve(left), cons, left[1], own[1], wall_low)
            for f in range(5):
                change[f] = change[f] - flux[f]
            flux = face(cons, conserve(right), own[1], right[1], wall_high)
            for f in range(5):
                change[f] = change[f] + flux[f]
            fresh = [cons[f] - step_ratio * change[f] for f in range(5)]
            scale = 1.0 / fresh[0]
            out = pl.ds(z * height + y0, chunk)
            adv_ref[0, out, :] = fresh[0]
            for f in range(1, 5):
                adv_ref[f, out, :] = fresh[f] * scale
        return carry

    lax.fori_loop(0, depth, plane, 0)

    def pick(s, carry):
        for r in range(cap):
            b = jnp.maximum(map_ref[0, s * cap + r], 0)
            for f in range(5):
                picked[s, f * cap + r : f * cap + r + 1, :] = adv_ref[f, pl.ds(b, 1), :]
        return carry

    lax.fori_loop(0, n, pick, 0)

    def part(ref, s, j):
        return ref[s, j * cap : (j + 1) * cap, :]

    def couple(ref, s):
        g = part(picked, s, 0)
        scale = 1.0 / (g + part(ref, s, 0))
        for c in range(3):
            new_ref[s, c * cap : (c + 1) * cap, :] = (
                g * part(picked, s, 1 + c) + part(ref, s, 1 + c)
            ) * scale
        new_ref[s, 3 * cap : 4 * cap, :] = (g * part(picked, s, 4) + part(ref, s, 4)) / (
            g + part(ref, s, 5)
        )

    couple(pay_ref, me)
    home[me] = new_ref[me]

    def inward(k):
        d = lax.rem(me + n - k, n)
        return pltpu.make_async_remote_copy(
            src_ref=new_ref.at[d],
            dst_ref=home.at[me],
            send_sem=back_send.at[k],
            recv_sem=back_recv.at[k],
            device_id=place(d),
            device_id_type=MESH,
        )

    def answer(k, carry):
        d = lax.rem(me + n - k, n)
        outward(k).wait()
        couple(got, d)
        inward(k).start()
        return carry

    lax.fori_loop(1, n, answer, 0)

    def finish(k, carry):
        inward(k).wait()
        return carry

    lax.fori_loop(1, n, finish, 0)
    ret_ref[...] = home[...]


def final_kernel(
    cap, rank_ref, map_ref, ex_ref, adv_ref, new_ref, ret_ref, sums_ref, out_ref, solid_ref
):
    slots = rank_ref.shape[0]
    positions = map_ref.shape[1]
    out_ref[...] = adv_ref[...]
    factor = [coefficients(ex_ref, m) for m in range(2)]

    def scatter(i, carry):
        for u in range(cap):
            b = map_ref[0, i * cap + u]

            @pl.when(b >= 0)
            def _(u=u, b=b):
                for j in range(back):
                    out_ref[1 + j, pl.ds(b, 1), :] = new_ref[i, j * cap + u : j * cap + u + 1, :]

        return carry

    lax.fori_loop(0, positions // cap, scatter, 0)

    def solid(k, carry):
        v = rank_ref[k]
        live = v >= 0
        v = jnp.maximum(v, 0)
        s = v // cap
        r = v % cap
        rows = [ret_ref[s, pl.ds(j * cap + r, 1), :] for j in range(back)]
        total = sums_ref[k]
        for m in range(2):
            mass = total[8 * m : 8 * m + 1]
            for j in range(back):
                fac = ex_ref[m, j // 3]
                value = (total[8 * m + 1 + j : 8 * m + 2 + j] + fac * rows[j]) / (mass + fac)
                solid_ref[j, pl.ds(2 * k + m, 1), :] = jnp.where(live, value, 0.0)
        return carry

    lax.fori_loop(0, slots, solid, 0)


def per_device(
    n_gx,
    n_gy,
    gaseous_rho,
    gaseous_flow_vector,
    gaseous_kelvin,
    sender_tile_map,
    receiver_arrival_rank,
    bin_active_number,
    grain_inertia,
    grain_motion_vector,
    grain_kelvin,
    grain_voxel_number,
    grain_substance_label,
    exchange_factor,
):
    n = n_gx * n_gy
    depth, height, width = gaseous_rho.shape
    slots = grain_inertia.shape[0]
    cap = sender_tile_map.shape[1] // n
    blocks = depth * height
    f32 = jnp.float32
    shape = jax.ShapeDtypeStruct
    pay, sums = pl.pallas_call(
        functools.partial(bin_kernel, cap),
        out_shape=(shape((n, sent * cap, width), f32), shape((slots, 16, width), f32)),
        in_specs=[SMEM] * 3 + [VMEM] * 5,
        out_specs=(VMEM, VMEM),
        compiler_params=pltpu.CompilerParams(vmem_limit_bytes=limit),
        name="bin_grains",
    )(
        receiver_arrival_rank,
        bin_active_number,
        exchange_factor,
        grain_inertia,
        grain_motion_vector,
        grain_kelvin,
        grain_voxel_number,
        grain_substance_label,
    )
    dma = pltpu.SemaphoreType.DMA
    adv, new, ret = pl.pallas_call(
        functools.partial(grid_kernel, n_gx, n_gy),
        out_shape=(
            shape((5, blocks, width), f32),
            shape((n, back * cap, width), f32),
            shape((n, back * cap, width), f32),
        ),
        in_specs=[SMEM] + [VMEM] * 4,
        out_specs=(VMEM,) * 3,
        scratch_shapes=[
            pltpu.VMEM((2, height, width), f32),
            pltpu.VMEM((2, height, width), f32),
            pltpu.VMEM((2, 5, depth, width), f32),
            pltpu.VMEM((2, 5, depth, width), f32),
            pltpu.VMEM((n, sent * cap, width), f32),
            pltpu.VMEM((n, back * cap, width), f32),
            pltpu.VMEM((6, height + 16, width), f32),
            pltpu.VMEM((5, height, width), f32),
            pltpu.VMEM((n, 5 * cap, width), f32),
            dma((4,)),
            dma((4,)),
            dma((n,)),
            dma((n,)),
            dma((n,)),
            dma((n,)),
        ],
        compiler_params=pltpu.CompilerParams(
            collective_id=0, has_side_effects=True, vmem_limit_bytes=limit
        ),
        name="advance_and_couple",
    )(sender_tile_map, gaseous_rho, gaseous_flow_vector, gaseous_kelvin, pay)
    final, solid = pl.pallas_call(
        functools.partial(final_kernel, cap),
        out_shape=(shape((5, blocks, width), f32), shape((back, 2 * slots, width), f32)),
        in_specs=[SMEM] * 3 + [VMEM] * 4,
        out_specs=(VMEM, VMEM),
        compiler_params=pltpu.CompilerParams(vmem_limit_bytes=limit),
        name="place_results",
    )(receiver_arrival_rank, sender_tile_map, exchange_factor, adv, new, ret, sums)
    return (
        final.reshape(5, depth, height, width),
        solid.reshape(back, slots, 2, width),
    )


def solution(mesh):
    placed = (
        P(None, "gy", "gx"),
        P(None, None, "gy", "gx"),
        P(None, "gy", "gx"),
        P(("gx", "gy"), None),
        P(("gx", "gy")),
        P(("gx", "gy")),
        P(("gx", "gy"), None),
        P(None, ("gx", "gy"), None),
        P(("gx", "gy"), None),
        P(("gx", "gy"), None),
        P(("gx", "gy"), None),
        P(),
    )
    return jax.shard_map(
        functools.partial(per_device, mesh.shape["gx"], mesh.shape["gy"]),
        mesh=mesh,
        in_specs=placed,
        out_specs=(P(None, None, "gy", "gx"), P(None, ("gx", "gy"), None, None)),
        check_vma=False,
    )
```

time: 246 us -> 71.7 us (0.29); the launches traced: 243 us -> 71.7 us
  other arithmetic: 109 us -> 0 us
  local copies, waits for them, and re-layouts: 76 us -> 0 us
  Pallas kernels: 0 us -> 71 us
  starting transfers between devices: 23.3 us -> 0 us
  matrix products: 17.4 us -> 0 us
  waiting for transfers between devices: 16.2 us -> 0 us
    pallas_call x0 -> x3, Pallas kernels: none -> 71 us  [the longest x1 47.4 us: per_device(): pl.pallas_call(functools.partial(grid_kernel, n_gx, n_gy), out_shape=(sha...]
    scatter-add x2 -> x0, other arithmetic: 24.6 us -> none  [the longest x1 17.6 us: per_device(): gains = jnp.zeros((4, block_count, width), jnp.float32).at[:, jnp.where(o...]
    slice x9 -> x0, local copies, waits for them, and re-layouts: 24.2 us -> none  [the longest x2 10.7 us: extended(): last = lax.slice_in_dim(array, length - width, length, axis=dim)]
    concatenate x7 -> x0, other arithmetic: 22 us -> none  [the longest x2 12 us: extended(): array = jnp.concatenate([before, array, after], axis=dim)]
    mul x7 -> x0, other arithmetic: 21 us -> none  [the longest x3 17.7 us: advance(): face_flux = face_speed * jnp.where(face_speed > 0, cons_lower, cons_upper)]
    sub x3 -> x0, other arithmetic: 17.5 us -> none  [the longest x1 14.7 us: advance(): updated = central - step_ratio * change]
    dot_general x4 -> x0, matrix products: 17.4 us -> none  [group_sum(): jnp.einsum('fsp,spc->fsc', group_values, onehot_table, precision=lax.Prec...]
    all_to_all x2 -> x0, waiting for transfers between devices: 16.2 us -> none  [the longest x1 13.5 us: per_device(): lax.all_to_all(outgoing.reshape(5, devices, capacity, width), ('gx', 'gy'...]
  transfers between devices with their start and end apart: 6 -> 0, of which waited for: 2 -> 0; matrix products, arithmetic and copies ran while one was open for 24% -> 0% of each run, Pallas kernels for 0% -> 0%
where the time goes in v1:
time: 71.7 us
  Pallas kernels  71 us (99%)
    pallas_call x1, Pallas kernels, per_device(): pl.pallas_call(functools.partial(grid_kernel, n_gx, n_gy), out_shape=(sha...  47.4 us
    pallas_call x1, Pallas kernels, per_device(): pl.pallas_call(functools.partial(bin_kernel, cap), out_shape=(shape((n, s...  15.1 us
    pallas_call x1, Pallas kernels, per_device(): pl.pallas_call(functools.partial(final_kernel, cap), out_shape=(shape((5,...  8.45 us

profile of v1, /device:TPU:0, one launch (start us, length us, event | category | flops | bytes accessed | tf_op | source)
XLA Modules:
  0.0 71.7 jit_solution(11164645389428180234)
XLA Ops:
  0.6 15.1 %bin_grains.1 = (f32[32,48,128]{2,1,0:T(8,128)}, f32[64,16,128]{2,1,0:T(8,128)}) custom-call(s32[64]{0:T(128)} %rank_ref.3, s32[64]{0:T(128)} %count_ref.1, f32[2,2]{1,0:T(2,128)} %ex_ref.3, f32[64,512]{1,0:T(8,128)} %mass_ref.1, f32[3,64,512]{2,1,0:T(8,128)} %vel_ref.2, f32[64,512]{1,0:T(8,128)} %temp_ref.2, s32[64,512]{1,0:T(8,128)} %vox_ref.1, ...), custom_call_target="tpu_custom_call" | custom-call | tf_op jit(solution)/shard_map/bin_grains/pallas_call | solution.py:415
  15.8 47.4 %advance_and_couple.1 = (f32[5,1536,128]{2,1,0:T(8,128)}, f32[32,32,128]{2,1,0:T(8,128)}, f32[32,32,128]{2,1,0:T(8,128)}) custom-call(s32[1,256]{1,0:T(1,128)} %map_ref.3, f32[16,96,128]{2,1,0:T(8,128)} %rho_ref.1, f32[3,16,96,128]{3,2,1,0:T(8,128)} %vel_ref.3, f32[16,96,128]{2,1,0:T(8,128)} %temp_ref.3, f32[32,48,128]{2,1,0:T(8,128)} %get-tuple-element.9.pay_ref), custom_call_target="tpu_custom_call" | custom-call | tf_op jit(solution)/shard_map/advance_and_couple/pallas_call | solution.py:433
  63.2 8.4 %place_results.1 = (f32[5,1536,128]{2,1,0:T(8,128)}, f32[4,128,128]{2,1,0:T(8,128)}) custom-call(s32[64]{0:T(128)} %rank_ref.3, s32[1,256]{1,0:T(1,128)} %map_ref.3, f32[2,2]{1,0:T(2,128)} %ex_ref.3, f32[5,1536,128]{2,1,0:T(8,128)} %get-tuple-element.10.adv_ref, f32[32,32,128]{2,1,0:T(8,128)} %get-tuple-element.11.new_ref, ...), custom_call_target="tpu_custom_call" | custom-call | tf_op jit(solution)/shard_map/place_results/pallas_call | solution.py:464

commit v2 on v1

--- a/solution.py
+++ b/solution.py
@@ -9,9 +9,10 @@
 
 MESH = pl.DeviceIdType.MESH
 VMEM = pl.BlockSpec(memory_space=pltpu.VMEM)
+ANY = pl.BlockSpec(memory_space=pl.ANY)
 SMEM = pl.BlockSpec(memory_space=pltpu.SMEM)
 step_ratio = 0.08
-limit = 56 * 1024 * 1024
+limit = 24 * 1024 * 1024
 sent = 6
 back = 4
 
@@ -22,7 +23,7 @@
 
 
 def bin_kernel(
-    cap, rank_ref, count_ref, ex_ref, mass_ref, vel_ref, temp_ref, vox_ref, lab_ref, pay_ref, sums_ref
+    cap, rank_ref, count_ref, ex_ref, mass_ref, vel_ref, temp_ref, vox_ref, lab_ref, pay_ref, calm_ref, pull_ref
 ):
     slots, padding = mass_ref.shape
     width = pay_ref.shape[2]
@@ -31,7 +32,8 @@
     lane = lax.broadcasted_iota(jnp.int32, (1, padding), 1)
     cells = lax.broadcasted_iota(jnp.int32, (width, padding), 0)
     factor = [coefficients(ex_ref, m) for m in range(2)]
-    unroll = 4
+    unroll = 8
+    spare = (pay_ref.shape[0] - 1) * cap
 
     def body(i, carry):
         for u in range(unroll):
@@ -56,19 +58,25 @@
                 preferred_element_type=jnp.float32,
             )
             total = total[:16] + total[16:]
-            sums_ref[k] = total
             pay = 0.0
+            v = rank_ref[k]
+            live = jnp.where(v >= 0, 1.0, 0.0)
             for m in range(2):
                 part = total[8 * m : 8 * m + 8]
-                pay = pay + factor[m] * part / (part[0:1] + factor[m])
-            v = rank_ref[k]
-
-            @pl.when(v >= 0)
-            def _():
-                s = v // cap
-                r = v % cap
-                for j in range(sent):
-                    pay_ref[s, pl.ds(j * cap + r, 1), :] = pay[j : j + 1]
+                scale = 1.0 / (part[0:1] + factor[m])
+                pull = factor[m] * scale
+                pay = pay + pull * part
+                calm = part * scale * live
+                pull = pull * live
+                for j in range(back):
+                    calm_ref[j, pl.ds(2 * k + m, 1), :] = calm[1 + j : 2 + j]
+                for j in range(2):
+                    pull_ref[j, pl.ds(2 * k + m, 1), :] = pull[1 + 3 * j : 2 + 3 * j]
+            v = jnp.where(v >= 0, v, spare)
+            s = v // cap
+            r = v % cap
+            for j in range(sent):
+                pay_ref[s, pl.ds(j * cap + r, 1), :] = pay[j : j + 1]
 
         return carry
 
@@ -350,43 +358,53 @@
 
 
 def final_kernel(
-    cap, rank_ref, map_ref, ex_ref, adv_ref, new_ref, ret_ref, sums_ref, out_ref, solid_ref
+    cap, rank_ref, map_ref, adv_ref, new_ref, ret_ref, calm_ref, pull_ref, out_ref, solid_ref, held, sem
 ):
     slots = rank_ref.shape[0]
     positions = map_ref.shape[1]
-    out_ref[...] = adv_ref[...]
-    factor = [coefficients(ex_ref, m) for m in range(2)]
+    fields, blocks, width = adv_ref.shape
+
+    def whole(f, inward):
+        here = held.at[f, pl.ds(0, blocks), :]
+        if inward:
+            return pltpu.make_async_copy(adv_ref.at[f], here, sem.at[f])
+        return pltpu.make_async_copy(here, out_ref.at[f], sem.at[f])
+
+    for f in range(fields):
+        whole(f, True).start()
+    unroll = 8
+
+    def solid(i, carry):
+        for u in range(unroll):
+            k = i * unroll + u
+            v = jnp.maximum(rank_ref[k], 0)
+            s = v // cap
+            r = v % cap
+            for j in range(back):
+                row = ret_ref[s, pl.ds(j * cap + r, 1), :]
+                solid_ref[j, pl.ds(2 * k, 2), :] = jnp.broadcast_to(row, (2, width))
+        return carry
+
+    lax.fori_loop(0, slots // unroll, solid, 0)
+    for j in range(back):
+        solid_ref[j] = calm_ref[j] + pull_ref[j // 3] * solid_ref[j]
+    for f in range(fields):
+        whole(f, True).wait()
+    whole(0, False).start()
 
     def scatter(i, carry):
         for u in range(cap):
             b = map_ref[0, i * cap + u]
-
-            @pl.when(b >= 0)
-            def _(u=u, b=b):
-                for j in range(back):
-                    out_ref[1 + j, pl.ds(b, 1), :] = new_ref[i, j * cap + u : j * cap + u + 1, :]
-
+            b = jnp.where(b >= 0, b, blocks)
+            for j in range(back):
+                held[1 + j, pl.ds(b, 1), :] = new_ref[i, j * cap + u : j * cap + u + 1, :]
         return carry
 
     lax.fori_loop(0, positions // cap, scatter, 0)
-
-    def solid(k, carry):
-        v = rank_ref[k]
-        live = v >= 0
-        v = jnp.maximum(v, 0)
-        s = v // cap
-        r = v % cap
-        rows = [ret_ref[s, pl.ds(j * cap + r, 1), :] for j in range(back)]
-        total = sums_ref[k]
-        for m in range(2):
-            mass = total[8 * m : 8 * m + 1]
-            for j in range(back):
-                fac = ex_ref[m, j // 3]
-                value = (total[8 * m + 1 + j : 8 * m + 2 + j] + fac * rows[j]) / (mass + fac)
-                solid_ref[j, pl.ds(2 * k + m, 1), :] = jnp.where(live, value, 0.0)
-        return carry
-
-    lax.fori_loop(0, slots, solid, 0)
+    for f in range(1, fields):
+        whole(f, False).start()
+    for f in range(fields):
+        whole(f, False).wait()
 
 
 def per_device(
@@ -412,11 +430,15 @@
     blocks = depth * height
     f32 = jnp.float32
     shape = jax.ShapeDtypeStruct
-    pay, sums = pl.pallas_call(
+    pay, calm, pull = pl.pallas_call(
         functools.partial(bin_kernel, cap),
-        out_shape=(shape((n, sent * cap, width), f32), shape((slots, 16, width), f32)),
+        out_shape=(
+            shape((n + 1, sent * cap, width), f32),
+            shape((back, 2 * slots, width), f32),
+            shape((2, 2 * slots, width), f32),
+        ),
         in_specs=[SMEM] * 3 + [VMEM] * 5,
-        out_specs=(VMEM, VMEM),
+        out_specs=(VMEM,) * 3,
         compiler_params=pltpu.CompilerParams(vmem_limit_bytes=limit),
         name="bin_grains",
     )(
@@ -464,11 +486,12 @@
     final, solid = pl.pallas_call(
         functools.partial(final_kernel, cap),
         out_shape=(shape((5, blocks, width), f32), shape((back, 2 * slots, width), f32)),
-        in_specs=[SMEM] * 3 + [VMEM] * 4,
-        out_specs=(VMEM, VMEM),
+        in_specs=[SMEM] * 2 + [ANY] + [VMEM] * 4,
+        out_specs=(ANY, VMEM),
+        scratch_shapes=[pltpu.VMEM((5, blocks + 8, width), f32), dma((5,))],
         compiler_params=pltpu.CompilerParams(vmem_limit_bytes=limit),
         name="place_results",
-    )(receiver_arrival_rank, sender_tile_map, exchange_factor, adv, new, ret, sums)
+    )(receiver_arrival_rank, sender_tile_map, adv, new, ret, calm, pull)
     return (
         final.reshape(5, depth, height, width),
         solid.reshape(back, slots, 2, width),

time: 71.7 us -> 64.4 us (0.90)
  Pallas kernels: 71 us -> 52.1 us
  local copies, waits for them, and re-layouts: 0 us -> 11.2 us
    unnamed x0 -> x28, local copies, waits for them, and re-layouts: none -> 11.2 us
    pallas_call x1, Pallas kernels: 15.1 us -> 4.42 us  [per_device(): pl.pallas_call(functools.partial(bin_kernel, cap), out_shape=(shape((n +...]
    pallas_call x1, Pallas kernels: 8.45 us -> 4.19 us  [per_device(): pl.pallas_call(functools.partial(final_kernel, cap), out_shape=(shape((5,...]
    pallas_call x1, Pallas kernels: 47.4 us -> 43.5 us  [per_device(): pl.pallas_call(functools.partial(grid_kernel, n_gx, n_gy), out_shape=(sha...]
where the time goes in v2:
time: 64.4 us; the launch traced here: 64 us
  Pallas kernels  52.1 us (81%)
  local copies, waits for them, and re-layouts  11.2 us (17%)
  between operations  0.69 us (1%)
    pallas_call x1, Pallas kernels, per_device(): pl.pallas_call(functools.partial(grid_kernel, n_gx, n_gy), out_shape=(sha...  43.5 us
    unnamed x28, local copies, waits for them, and re-layouts  11.2 us
    pallas_call x1, Pallas kernels, per_device(): pl.pallas_call(functools.partial(bin_kernel, cap), out_shape=(shape((n +...  4.42 us
    pallas_call x1, Pallas kernels, per_device(): pl.pallas_call(functools.partial(final_kernel, cap), out_shape=(shape((5,...  4.19 us

profile of v2, /device:TPU:0, one launch (start us, length us, event | category | flops | bytes accessed | tf_op | source)
XLA Modules:
  0.0 64.0 jit_solution(10972710401586521621)
XLA Ops:
  0.6 0.0 copy-start.3
  0.6 1.0 %copy-done.3 = f32[3,64,512]{2,1,0:T(8,128)S(1)} copy-done((f32[3,64,512]{2,1,0:T(8,128)S(1)}, f32[3,64,512]{2,1,0:T(8,128)}, u32[]{:S(2)}) %copy-start.3) | copy-done | bytes 393240
  1.6 0.0 copy-start.4
  1.6 0.9 %copy-done.4 = f32[64,512]{1,0:T(8,128)S(1)} copy-done((f32[64,512]{1,0:T(8,128)S(1)}, f32[64,512]{1,0:T(8,128)}, u32[]{:S(2)}) %copy-start.4) | copy-done | bytes 131096
  2.5 0.0 copy-start.5
  2.5 0.9 %copy-done.5 = f32[64,512]{1,0:T(8,128)S(1)} copy-done((f32[64,512]{1,0:T(8,128)S(1)}, f32[64,512]{1,0:T(8,128)}, u32[]{:S(2)}) %copy-start.5) | copy-done | bytes 131096
  3.4 0.9 %copy-done.6 = s32[64,512]{1,0:T(8,128)S(1)} copy-done((s32[64,512]{1,0:T(8,128)S(1)}, s32[64,512]{1,0:T(8,128)}, u32[]{:S(2)}) %copy-start.6) | copy-done | bytes 131096
  4.3 0.0 copy-start.7
  4.3 0.9 %copy-done.7 = s32[64,512]{1,0:T(8,128)S(1)} copy-done((s32[64,512]{1,0:T(8,128)S(1)}, s32[64,512]{1,0:T(8,128)}, u32[]{:S(2)}) %copy-start.7) | copy-done | bytes 131096
  5.2 0.0 copy-start.10
  5.3 0.7 %copy-done.10 = s32[64]{0:T(128)S(1)} copy-done((s32[64]{0:T(128)S(1)}, s32[64]{0:T(128)}, u32[]{:S(2)}) %copy-start.10) | copy-done | bytes 280
  5.9 0.0 copy-start.12
  5.9 0.7 %copy-done.12 = f32[2,2]{1,0:T(2,128)S(1)} copy-done((f32[2,2]{1,0:T(2,128)S(1)}, f32[2,2]{1,0:T(2,128)}, u32[]{:S(2)}) %copy-start.12) | copy-done | bytes 40
  6.6 0.7 %copy-done.13 = s32[64]{0:T(128)S(1)} copy-done((s32[64]{0:T(128)S(1)}, s32[64]{0:T(128)}, u32[]{:S(2)}) %copy-start.13) | copy-done | bytes 280
  7.2 4.4 %bin_grains.1 = (f32[33,48,128]{2,1,0:T(8,128)S(1)}, f32[4,128,128]{2,1,0:T(8,128)S(1)}, f32[2,128,128]{2,1,0:T(8,128)S(1)}) custom-call(s32[64]{0:T(128)S(1)} %copy-done.10, s32[64]{0:T(128)S(1)} %copy-done.13, f32[2,2]{1,0:T(2,128)S(1)} %copy-done.12, f32[64,512]{1,0:T(8,128)S(1)} %copy-done.4, f32[3,64,512]{2,1,0:T(8,128)S(1)} %copy-done.3, ...), custom_call_target="tpu_custom_call" | custom-call | tf_op jit(solution)/shard_map/bin_grains/pallas_call | solution.py:433
  11.7 0.0 copy-start
  11.7 1.7 %copy-done = f32[3,16,96,128]{3,2,1,0:T(8,128)S(1)} copy-done((f32[3,16,96,128]{3,2,1,0:T(8,128)S(1)}, f32[3,16,96,128]{3,2,1,0:T(8,128)}, u32[]{:S(2)}) %copy-start) | copy-done | bytes 2359320
  13.3 1.1 %copy-done.1 = f32[16,96,128]{2,1,0:T(8,128)S(1)} copy-done((f32[16,96,128]{2,1,0:T(8,128)S(1)}, f32[16,96,128]{2,1,0:T(8,128)}, u32[]{:S(2)}) %copy-start.1) | copy-done | bytes 786456
  14.5 1.1 %copy-done.2 = f32[16,96,128]{2,1,0:T(8,128)S(1)} copy-done((f32[16,96,128]{2,1,0:T(8,128)S(1)}, f32[16,96,128]{2,1,0:T(8,128)}, u32[]{:S(2)}) %copy-start.2) | copy-done | bytes 786456
  15.6 0.7 %copy-done.8 = s32[1,256]{1,0:T(1,128)S(1)} copy-done((s32[1,256]{1,0:T(1,128)S(1)}, s32[1,256]{1,0:T(1,128)}, u32[]{:S(2)}) %copy-start.8) | copy-done | bytes 1048
  16.3 43.5 %advance_and_couple.1 = (f32[5,1536,128]{2,1,0:T(8,128)S(1)}, f32[32,32,128]{2,1,0:T(8,128)S(1)}, f32[32,32,128]{2,1,0:T(8,128)S(1)}) custom-call(s32[1,256]{1,0:T(1,128)S(1)} %copy-done.8, f32[16,96,128]{2,1,0:T(8,128)S(1)} %copy-done.1, f32[3,16,96,128]{3,2,1,0:T(8,128)S(1)} %copy-done, f32[16,96,128]{2,1,0:T(8,128)S(1)} %copy-done.2, ...), custom_call_target="tpu_custom_call" | custom-call | tf_op jit(solution)/shard_map/advance_and_couple/pallas_call | solution.py:455
  59.8 0.0 copy-done.9
  59.8 0.0 copy-done.11
  59.8 4.2 %place_results.1 = (f32[5,1536,128]{2,1,0:T(8,128)}, f32[4,128,128]{2,1,0:T(8,128)}) custom-call(s32[64]{0:T(128)S(1)} %copy-done.11, s32[1,256]{1,0:T(1,128)S(1)} %copy-done.9, f32[5,1536,128]{2,1,0:T(8,128)S(1)} %get-tuple-element.11.adv_ref, f32[32,32,128]{2,1,0:T(8,128)S(1)} %get-tuple-element.12.new_ref, f32[32,32,128]{2,1,0:T(8,128)S(1)} %get-tuple-element.13.ret_ref, ...), custom_call_target="tpu_custom_call" | custom-call | tf_op jit(solution)/shard_map/place_results/pallas_call | solution.py:486
  (7 shorter events, 0.0 us)
Async XLA Ops:
  0.6 1.0 %copy-start.3 = (f32[3,64,512]{2,1,0:T(8,128)S(1)}, f32[3,64,512]{2,1,0:T(8,128)}, u32[]{:S(2)}) copy-start(f32[3,64,512]{2,1,0:T(8,128)} %vel_ref.2) | copy-start | bytes 1179652
  1.6 0.9 %copy-start.4 = (f32[64,512]{1,0:T(8,128)S(1)}, f32[64,512]{1,0:T(8,128)}, u32[]{:S(2)}) copy-start(f32[64,512]{1,0:T(8,128)} %mass_ref.1) | copy-start | bytes 393220
  2.5 0.9 %copy-start.5 = (f32[64,512]{1,0:T(8,128)S(1)}, f32[64,512]{1,0:T(8,128)}, u32[]{:S(2)}) copy-start(f32[64,512]{1,0:T(8,128)} %temp_ref.2) | copy-start | bytes 393220
  3.4 0.9 %copy-start.6 = (s32[64,512]{1,0:T(8,128)S(1)}, s32[64,512]{1,0:T(8,128)}, u32[]{:S(2)}) copy-start(s32[64,512]{1,0:T(8,128)} %vox_ref.1) | copy-start | bytes 393220
  4.3 0.9 %copy-start.7 = (s32[64,512]{1,0:T(8,128)S(1)}, s32[64,512]{1,0:T(8,128)}, u32[]{:S(2)}) copy-start(s32[64,512]{1,0:T(8,128)} %lab_ref.1) | copy-start | bytes 393220
  5.2 0.7 %copy-start.10 = (s32[64]{0:T(128)S(1)}, s32[64]{0:T(128)}, u32[]{:S(2)}) copy-start(s32[64]{0:T(128)} %rank_ref.3) | copy-start | bytes 772
  5.9 0.7 %copy-start.12 = (f32[2,2]{1,0:T(2,128)S(1)}, f32[2,2]{1,0:T(2,128)}, u32[]{:S(2)}) copy-start(f32[2,2]{1,0:T(2,128)} %ex_ref.1) | copy-start | bytes 52
  6.6 0.7 %copy-start.13 = (s32[64]{0:T(128)S(1)}, s32[64]{0:T(128)}, u32[]{:S(2)}) copy-start(s32[64]{0:T(128)} %count_ref.1) | copy-start | bytes 772
  7.2 52.6 %copy-start.9 = (s32[1,256]{1,0:T(1,128)S(1)}, s32[1,256]{1,0:T(1,128)}, u32[]{:S(2)}) copy-start(s32[1,256]{1,0:T(1,128)} %map_ref.3) | copy-start | bytes 3076
  7.2 52.6 %copy-start.11 = (s32[64]{0:T(128)S(1)}, s32[64]{0:T(128)}, u32[]{:S(2)}) copy-start(s32[64]{0:T(128)} %rank_ref.3) | copy-start | bytes 772
  11.7 1.7 %copy-start = (f32[3,16,96,128]{3,2,1,0:T(8,128)S(1)}, f32[3,16,96,128]{3,2,1,0:T(8,128)}, u32[]{:S(2)}) copy-start(f32[3,16,96,128]{3,2,1,0:T(8,128)} %vel_ref.3) | copy-start | bytes 7077892
  13.3 1.1 %copy-start.1 = (f32[16,96,128]{2,1,0:T(8,128)S(1)}, f32[16,96,128]{2,1,0:T(8,128)}, u32[]{:S(2)}) copy-start(f32[16,96,128]{2,1,0:T(8,128)} %rho_ref.1) | copy-start | bytes 2359300
  14.5 1.1 %copy-start.2 = (f32[16,96,128]{2,1,0:T(8,128)S(1)}, f32[16,96,128]{2,1,0:T(8,128)}, u32[]{:S(2)}) copy-start(f32[16,96,128]{2,1,0:T(8,128)} %temp_ref.3) | copy-start | bytes 2359300
  15.6 0.7 %copy-start.8 = (s32[1,256]{1,0:T(1,128)S(1)}, s32[1,256]{1,0:T(1,128)}, u32[]{:S(2)}) copy-start(s32[1,256]{1,0:T(1,128)} %map_ref.3) | copy-start | bytes 3076

commit v3 on v2

--- a/solution.py
+++ b/solution.py
@@ -9,6 +9,7 @@
 
 MESH = pl.DeviceIdType.MESH
 VMEM = pl.BlockSpec(memory_space=pltpu.VMEM)
+HBM = pl.BlockSpec(memory_space=pltpu.HBM)
 ANY = pl.BlockSpec(memory_space=pl.ANY)
 SMEM = pl.BlockSpec(memory_space=pltpu.SMEM)
 step_ratio = 0.08
@@ -22,24 +23,22 @@
     return jnp.where(rows < 4, ex_ref[m, 0], ex_ref[m, 1])
 
 
-def bin_kernel(
-    cap, rank_ref, count_ref, ex_ref, mass_ref, vel_ref, temp_ref, vox_ref, lab_ref, pay_ref, calm_ref, pull_ref
+def bin_grains(
+    rank_ref, count_ref, ex_ref, mass_ref, vel_ref, temp_ref, vox_ref, lab_ref, dense, calm_ref, pull_ref
 ):
     slots, padding = mass_ref.shape
-    width = pay_ref.shape[2]
-    pay_ref[...] = jnp.zeros_like(pay_ref)
+    width = dense.shape[2]
     rows = lax.broadcasted_iota(jnp.int32, (8, padding), 0)
     lane = lax.broadcasted_iota(jnp.int32, (1, padding), 1)
     cells = lax.broadcasted_iota(jnp.int32, (width, padding), 0)
     factor = [coefficients(ex_ref, m) for m in range(2)]
     unroll = 8
-    spare = (pay_ref.shape[0] - 1) * cap
 
     def body(i, carry):
         for u in range(unroll):
             k = i * unroll + u
             here = pl.ds(k, 1)
-            mass = jnp.where(lane < count_ref[k], mass_ref[here, :], 0.0)
+            mass = jnp.where(lane < count_ref[0, k], mass_ref[here, :], 0.0)
             base = jnp.where(rows == 4, temp_ref[here, :], 1.0)
             for c in range(3):
                 base = jnp.where(rows == c + 1, vel_ref[c, here, :], base)
@@ -48,19 +47,16 @@
             values = jnp.concatenate(
                 [jnp.where(label == 0, base, 0.0), jnp.where(label == 1, base, 0.0)], 0
             )
-            high = values.astype(jnp.bfloat16)
-            low = (values - high.astype(jnp.float32)).astype(jnp.bfloat16)
             onehot = jnp.where(cells == vox_ref[here, :], 1.0, 0.0).astype(jnp.bfloat16)
             total = lax.dot_general(
-                jnp.concatenate([high, low], 0),
+                jnp.concatenate(split(values, 2), 0),
                 onehot,
                 (((1,), (1,)), ((), ())),
                 preferred_element_type=jnp.float32,
             )
             total = total[:16] + total[16:]
             pay = 0.0
-            v = rank_ref[k]
-            live = jnp.where(v >= 0, 1.0, 0.0)
+            live = jnp.where(rank_ref[0, k] >= 0, 1.0, 0.0)
             for m in range(2):
                 part = total[8 * m : 8 * m + 8]
                 scale = 1.0 / (part[0:1] + factor[m])
@@ -72,15 +68,32 @@
                     calm_ref[j, pl.ds(2 * k + m, 1), :] = calm[1 + j : 2 + j]
                 for j in range(2):
                     pull_ref[j, pl.ds(2 * k + m, 1), :] = pull[1 + 3 * j : 2 + 3 * j]
-            v = jnp.where(v >= 0, v, spare)
-            s = v // cap
-            r = v % cap
             for j in range(sent):
-                pay_ref[s, pl.ds(j * cap + r, 1), :] = pay[j : j + 1]
-
+                dense[j, here, :] = pay[j : j + 1]
         return carry
 
     lax.fori_loop(0, slots // unroll, body, 0)
+
+
+def split(x, parts):
+    out = []
+    for _ in range(parts):
+        out.append(x.astype(jnp.bfloat16))
+        x = x - out[-1].astype(jnp.float32)
+    return out
+
+
+def place_pay(rank_row, dense, pay_ref, cap):
+    n = pay_ref.shape[0]
+    slots = dense.shape[1]
+    position = lax.broadcasted_iota(jnp.int32, (n * cap, slots), 0)
+    onehot = jnp.where(position == rank_row[...], 1.0, 0.0).astype(jnp.bfloat16)
+    for j in range(sent):
+        total = 0.0
+        for piece in split(dense[j], 3):
+            total = total + jnp.dot(onehot, piece, preferred_element_type=jnp.float32)
+        for s in range(n):
+            pay_ref[s, j * cap : (j + 1) * cap, :] = total[s * cap : (s + 1) * cap]
 
 
 def face(a, b, ua, ub, wall):
@@ -98,14 +111,38 @@
 def grid_kernel(
     n_gx,
     n_gy,
-    map_ref,
+    rho_hbm,
+    vel_hbm,
+    temp_hbm,
+    map_hbm,
+    rank_hbm,
+    count_hbm,
+    mass_hbm,
+    motion_hbm,
+    kelvin_hbm,
+    vox_hbm,
+    lab_hbm,
+    ex_hbm,
+    adv_ref,
+    new_ref,
+    ret_ref,
+    calm_ref,
+    pull_ref,
     rho_ref,
     vel_ref,
     temp_ref,
+    mass_ref,
+    motion_ref,
+    kelvin_ref,
+    vox_ref,
+    lab_ref,
+    rank_row,
+    map_ref,
+    rank_ref,
+    count_ref,
+    ex_ref,
+    dense,
     pay_ref,
-    adv_ref,
-    new_ref,
-    ret_ref,
     xsend,
     xrecv,
     ysend,
@@ -115,6 +152,7 @@
     ext,
     flux_z,
     picked,
+    load_sem,
     halo_send,
     halo_recv,
     pay_send,
@@ -124,7 +162,7 @@
 ):
     n = n_gx * n_gy
     depth, height, width = rho_ref.shape
-    cap = map_ref.shape[1] // n
+    cap = map_hbm.shape[1] // n
     gx = lax.axis_index("gx")
     gy = lax.axis_index("gy")
     me = gx * n_gy + gy
@@ -132,6 +170,14 @@
     def place(d):
         return (d // n_gy, lax.rem(d, n_gy))
 
+    def ahead(k):
+        x = lax.rem(gx + lax.rem(k, n_gx), n_gx)
+        return x * n_gy + lax.rem(gy + k // n_gx, n_gy)
+
+    def behind(k):
+        x = lax.rem(gx + n_gx - lax.rem(k, n_gx), n_gx)
+        return x * n_gy + lax.rem(gy + n_gy - k // n_gx, n_gy)
+
     barrier = pltpu.get_barrier_semaphore()
 
     def greet(k, carry):
@@ -139,7 +185,31 @@
         pl.semaphore_signal(barrier, inc=1, device_id=place(d), device_id_type=MESH)
         return carry
 
+    loads = [
+        pltpu.make_async_copy(src, dst, load_sem.at[i])
+        for i, (src, dst) in enumerate(
+            (
+                (rho_hbm, rho_ref),
+                (vel_hbm, vel_ref),
+                (temp_hbm, temp_ref),
+                (mass_hbm, mass_ref),
+                (motion_hbm, motion_ref),
+                (kelvin_hbm, kelvin_ref),
+                (vox_hbm, vox_ref),
+                (lab_hbm, lab_ref),
+                (rank_hbm, rank_row),
+                (map_hbm, map_ref),
+                (rank_hbm, rank_ref),
+                (count_hbm, count_ref),
+                (ex_hbm, ex_ref),
+            )
+        )
+    ]
+    for load in loads:
+        load.start()
     lax.fori_loop(1, n, greet, 0)
+    for load in loads[:3]:
+        load.wait()
 
     def prim(f, z, rows):
         if f == 0:
@@ -191,8 +261,25 @@
         def _(which=which, side=side, device=device):
             halo(which, side, device).start()
 
+    for load in loads[3:]:
+        load.wait()
+    bin_grains(
+        rank_ref,
+        count_ref,
+        ex_ref,
+        mass_ref,
+        motion_ref,
+        kelvin_ref,
+        vox_ref,
+        lab_ref,
+        dense,
+        calm_ref,
+        pull_ref,
+    )
+    place_pay(rank_row, dense, pay_ref, cap)
+
     def outward(k):
-        d = lax.rem(me + k, n)
+        d = ahead(k)
         return pltpu.make_async_remote_copy(
             src_ref=pay_ref.at[d],
             dst_ref=got.at[me],
@@ -330,7 +417,7 @@
     home[me] = new_ref[me]
 
     def inward(k):
-        d = lax.rem(me + n - k, n)
+        d = behind(k)
         return pltpu.make_async_remote_copy(
             src_ref=new_ref.at[d],
             dst_ref=home.at[me],
@@ -341,7 +428,7 @@
         )
 
     def answer(k, carry):
-        d = lax.rem(me + n - k, n)
+        d = behind(k)
         outward(k).wait()
         couple(got, d)
         inward(k).start()
@@ -425,43 +512,39 @@
 ):
     n = n_gx * n_gy
     depth, height, width = gaseous_rho.shape
-    slots = grain_inertia.shape[0]
+    slots, padding = grain_inertia.shape
     cap = sender_tile_map.shape[1] // n
     blocks = depth * height
-    f32 = jnp.float32
+    f32, i32 = jnp.float32, jnp.int32
     shape = jax.ShapeDtypeStruct
-    pay, calm, pull = pl.pallas_call(
-        functools.partial(bin_kernel, cap),
-        out_shape=(
-            shape((n + 1, sent * cap, width), f32),
-            shape((back, 2 * slots, width), f32),
-            shape((2, 2 * slots, width), f32),
-        ),
-        in_specs=[SMEM] * 3 + [VMEM] * 5,
-        out_specs=(VMEM,) * 3,
-        compiler_params=pltpu.CompilerParams(vmem_limit_bytes=limit),
-        name="bin_grains",
-    )(
-        receiver_arrival_rank,
-        bin_active_number,
-        exchange_factor,
-        grain_inertia,
-        grain_motion_vector,
-        grain_kelvin,
-        grain_voxel_number,
-        grain_substance_label,
-    )
     dma = pltpu.SemaphoreType.DMA
-    adv, new, ret = pl.pallas_call(
+    adv, new, ret, calm, pull = pl.pallas_call(
         functools.partial(grid_kernel, n_gx, n_gy),
         out_shape=(
             shape((5, blocks, width), f32),
             shape((n, back * cap, width), f32),
             shape((n, back * cap, width), f32),
+            shape((back, 2 * slots, width), f32),
+            shape((2, 2 * slots, width), f32),
         ),
-        in_specs=[SMEM] + [VMEM] * 4,
-        out_specs=(VMEM,) * 3,
+        in_specs=[HBM] * 12,
+        out_specs=(VMEM,) * 5,
         scratch_shapes=[
+            pltpu.VMEM((depth, height, width), f32),
+            pltpu.VMEM((3, depth, height, width), f32),
+            pltpu.VMEM((depth, height, width), f32),
+            pltpu.VMEM((slots, padding), f32),
+            pltpu.VMEM((3, slots, padding), f32),
+            pltpu.VMEM((slots, padding), f32),
+            pltpu.VMEM((slots, padding), i32),
+            pltpu.VMEM((slots, padding), i32),
+            pltpu.VMEM((1, slots), i32),
+            pltpu.SMEM((1, n * cap), i32),
+            pltpu.SMEM((1, slots), i32),
+            pltpu.SMEM((1, slots), i32),
+            pltpu.SMEM((2, 2), f32),
+            pltpu.VMEM((sent, slots, width), f32),
+            pltpu.VMEM((n, sent * cap, width), f32),
             pltpu.VMEM((2, height, width), f32),
             pltpu.VMEM((2, height, width), f32),
             pltpu.VMEM((2, 5, depth, width), f32),
@@ -471,6 +554,7 @@
             pltpu.VMEM((6, height + 16, width), f32),
             pltpu.VMEM((5, height, width), f32),
             pltpu.VMEM((n, 5 * cap, width), f32),
+            dma((13,)),
             dma((4,)),
             dma((4,)),
             dma((n,)),
@@ -482,7 +566,20 @@
             collective_id=0, has_side_effects=True, vmem_limit_bytes=limit
         ),
         name="advance_and_couple",
-    )(sender_tile_map, gaseous_rho, gaseous_flow_vector, gaseous_kelvin, pay)
+    )(
+        gaseous_rho,
+        gaseous_flow_vector,
+        gaseous_kelvin,
+        sender_tile_map,
+        receiver_arrival_rank.reshape(1, slots),
+        bin_active_number.reshape(1, slots),
+        grain_inertia,
+        grain_motion_vector,
+        grain_kelvin,
+        grain_voxel_number,
+        grain_substance_label,
+        exchange_factor,
+    )
     final, solid = pl.pallas_call(
         functools.partial(final_kernel, cap),
         out_shape=(shape((5, blocks, width), f32), shape((back, 2 * slots, width), f32)),

time: 64.4 us -> 61.3 us (0.952)
  Pallas kernels: 52.1 us -> 49 us
    pallas_call x1 -> x0, Pallas kernels: 4.42 us -> none  [per_device(): pl.pallas_call(functools.partial(bin_kernel, cap), out_shape=(shape((n +...]
    pallas_call x1, Pallas kernels: 43.5 us -> 44.8 us  [per_device(): pl.pallas_call(functools.partial(grid_kernel, n_gx, n_gy), out_shape=(sha...]
    unnamed x28 -> x24, local copies, waits for them, and re-layouts: 11.2 us -> 11.2 us
where the time goes in v3:
time: 61.3 us; the launch traced here: 60.9 us
  Pallas kernels  49 us (80%)
  local copies, waits for them, and re-layouts  11.2 us (18%)
  between operations  0.66 us (1%)
    pallas_call x1, Pallas kernels, per_device(): pl.pallas_call(functools.partial(grid_kernel, n_gx, n_gy), out_shape=(sha...  44.8 us
    unnamed x24, local copies, waits for them, and re-layouts  11.2 us
    pallas_call x1, Pallas kernels, per_device(): pl.pallas_call(functools.partial(final_kernel, cap), out_shape=(shape((5,...  4.18 us

profile of v3, /device:TPU:0, one launch (start us, length us, event | category | flops | bytes accessed | tf_op | source)
XLA Modules:
  0.0 60.9 jit_solution(14991232157194470660)
XLA Ops:
  0.6 0.0 copy-start
  0.6 1.7 %copy-done = f32[3,16,96,128]{3,2,1,0:T(8,128)S(1)} copy-done((f32[3,16,96,128]{3,2,1,0:T(8,128)S(1)}, f32[3,16,96,128]{3,2,1,0:T(8,128)}, u32[]{:S(2)}) %copy-start) | copy-done | bytes 2359320
  2.3 0.0 copy-start.1
  2.3 1.1 %copy-done.1 = f32[16,96,128]{2,1,0:T(8,128)S(1)} copy-done((f32[16,96,128]{2,1,0:T(8,128)S(1)}, f32[16,96,128]{2,1,0:T(8,128)}, u32[]{:S(2)}) %copy-start.1) | copy-done | bytes 786456
  3.4 0.0 copy-start.2
  3.4 1.1 %copy-done.2 = f32[16,96,128]{2,1,0:T(8,128)S(1)} copy-done((f32[16,96,128]{2,1,0:T(8,128)S(1)}, f32[16,96,128]{2,1,0:T(8,128)}, u32[]{:S(2)}) %copy-start.2) | copy-done | bytes 786456
  4.6 0.0 copy-start.3
  4.6 1.0 %copy-done.3 = f32[3,64,512]{2,1,0:T(8,128)S(1)} copy-done((f32[3,64,512]{2,1,0:T(8,128)S(1)}, f32[3,64,512]{2,1,0:T(8,128)}, u32[]{:S(2)}) %copy-start.3) | copy-done | bytes 393240
  5.6 0.0 copy-start.4
  5.6 0.9 %copy-done.4 = f32[64,512]{1,0:T(8,128)S(1)} copy-done((f32[64,512]{1,0:T(8,128)S(1)}, f32[64,512]{1,0:T(8,128)}, u32[]{:S(2)}) %copy-start.4) | copy-done | bytes 131096
  6.5 0.9 %copy-done.5 = f32[64,512]{1,0:T(8,128)S(1)} copy-done((f32[64,512]{1,0:T(8,128)S(1)}, f32[64,512]{1,0:T(8,128)}, u32[]{:S(2)}) %copy-start.5) | copy-done | bytes 131096
  7.4 0.0 copy-start.6
  7.4 0.9 %copy-done.6 = s32[64,512]{1,0:T(8,128)S(1)} copy-done((s32[64,512]{1,0:T(8,128)S(1)}, s32[64,512]{1,0:T(8,128)}, u32[]{:S(2)}) %copy-start.6) | copy-done | bytes 131096
  8.3 0.0 copy-start.7
  8.3 0.9 %copy-done.7 = s32[64,512]{1,0:T(8,128)S(1)} copy-done((s32[64,512]{1,0:T(8,128)S(1)}, s32[64,512]{1,0:T(8,128)}, u32[]{:S(2)}) %copy-start.7) | copy-done | bytes 131096
  9.2 0.0 copy-start.8
  9.2 0.7 %copy-done.8 = s32[1,256]{1,0:T(1,128)S(1)} copy-done((s32[1,256]{1,0:T(1,128)S(1)}, s32[1,256]{1,0:T(1,128)}, u32[]{:S(2)}) %copy-start.8) | copy-done | bytes 1048
  9.9 0.0 copy-start.9
  9.9 0.7 %copy-done.9 = s32[64]{0:T(128)S(1)} copy-done((s32[64]{0:T(128)S(1)}, s32[64]{0:T(128)}, u32[]{:S(2)}) %copy-start.9) | copy-done | bytes 280
  10.5 0.0 copy-start.10
  10.5 0.7 %copy-done.10 = f32[2,2]{1,0:T(2,128)S(1)} copy-done((f32[2,2]{1,0:T(2,128)S(1)}, f32[2,2]{1,0:T(2,128)}, u32[]{:S(2)}) %copy-start.10) | copy-done | bytes 40
  11.2 0.7 %copy-done.11 = s32[64]{0:T(128)S(1)} copy-done((s32[64]{0:T(128)S(1)}, s32[64]{0:T(128)}, u32[]{:S(2)}) %copy-start.11) | copy-done | bytes 280
  11.9 44.8 %advance_and_couple.1 = (f32[5,1536,128]{2,1,0:T(8,128)S(1)}, f32[32,32,128]{2,1,0:T(8,128)S(1)}, f32[32,32,128]{2,1,0:T(8,128)S(1)}, f32[4,128,128]{2,1,0:T(8,128)S(1)}, f32[2,128,128]{2,1,0:T(8,128)S(1)}) custom-call(f32[16,96,128]{2,1,0:T(8,128)S(1)} %copy-done.1, f32[3,16,96,128]{3,2,1,0:T(8,128)S(1)} %copy-done, f32[16,96,128]{2,1,0:T(8,128)S(1)} %copy-done.2, ...), custom_call_target="tpu_custom_call" | custom-call | tf_op jit(solution)/shard_map/advance_and_couple/pallas_call | solution.py:521
  56.7 4.2 %place_results.1 = (f32[5,1536,128]{2,1,0:T(8,128)}, f32[4,128,128]{2,1,0:T(8,128)}) custom-call(s32[64]{0:T(128)S(1)} %copy-done.9, s32[1,256]{1,0:T(1,128)S(1)} %copy-done.8, f32[5,1536,128]{2,1,0:T(8,128)S(1)} %get-tuple-element.9.adv_ref, f32[32,32,128]{2,1,0:T(8,128)S(1)} %get-tuple-element.10.new_ref, f32[32,32,128]{2,1,0:T(8,128)S(1)} %get-tuple-element.11.ret_ref, ...), custom_call_target="tpu_custom_call" | custom-call | tf_op jit(solution)/shard_map/place_results/pallas_call | solution.py:583
  (2 shorter events, 0.0 us)
Async XLA Ops:
  0.6 1.7 %copy-start = (f32[3,16,96,128]{3,2,1,0:T(8,128)S(1)}, f32[3,16,96,128]{3,2,1,0:T(8,128)}, u32[]{:S(2)}) copy-start(f32[3,16,96,128]{3,2,1,0:T(8,128)} %vel_hbm.1) | copy-start | bytes 7077892
  2.3 1.1 %copy-start.1 = (f32[16,96,128]{2,1,0:T(8,128)S(1)}, f32[16,96,128]{2,1,0:T(8,128)}, u32[]{:S(2)}) copy-start(f32[16,96,128]{2,1,0:T(8,128)} %rho_hbm.1) | copy-start | bytes 2359300
  3.4 1.1 %copy-start.2 = (f32[16,96,128]{2,1,0:T(8,128)S(1)}, f32[16,96,128]{2,1,0:T(8,128)}, u32[]{:S(2)}) copy-start(f32[16,96,128]{2,1,0:T(8,128)} %temp_hbm.1) | copy-start | bytes 2359300
  4.6 1.0 %copy-start.3 = (f32[3,64,512]{2,1,0:T(8,128)S(1)}, f32[3,64,512]{2,1,0:T(8,128)}, u32[]{:S(2)}) copy-start(f32[3,64,512]{2,1,0:T(8,128)} %motion_hbm.1) | copy-start | bytes 1179652
  5.6 0.9 %copy-start.4 = (f32[64,512]{1,0:T(8,128)S(1)}, f32[64,512]{1,0:T(8,128)}, u32[]{:S(2)}) copy-start(f32[64,512]{1,0:T(8,128)} %mass_hbm.1) | copy-start | bytes 393220
  6.5 0.9 %copy-start.5 = (f32[64,512]{1,0:T(8,128)S(1)}, f32[64,512]{1,0:T(8,128)}, u32[]{:S(2)}) copy-start(f32[64,512]{1,0:T(8,128)} %kelvin_hbm.1) | copy-start | bytes 393220
  7.4 0.9 %copy-start.6 = (s32[64,512]{1,0:T(8,128)S(1)}, s32[64,512]{1,0:T(8,128)}, u32[]{:S(2)}) copy-start(s32[64,512]{1,0:T(8,128)} %vox_hbm.1) | copy-start | bytes 393220
  8.3 0.9 %copy-start.7 = (s32[64,512]{1,0:T(8,128)S(1)}, s32[64,512]{1,0:T(8,128)}, u32[]{:S(2)}) copy-start(s32[64,512]{1,0:T(8,128)} %lab_hbm.1) | copy-start | bytes 393220
  9.2 0.7 %copy-start.8 = (s32[1,256]{1,0:T(1,128)S(1)}, s32[1,256]{1,0:T(1,128)}, u32[]{:S(2)}) copy-start(s32[1,256]{1,0:T(1,128)} %map_ref.1) | copy-start | bytes 3076
  9.9 0.7 %copy-start.9 = (s32[64]{0:T(128)S(1)}, s32[64]{0:T(128)}, u32[]{:S(2)}) copy-start(s32[64]{0:T(128)} %rank_ref.1) | copy-start | bytes 772
  10.5 0.7 %copy-start.10 = (f32[2,2]{1,0:T(2,128)S(1)}, f32[2,2]{1,0:T(2,128)}, u32[]{:S(2)}) copy-start(f32[2,2]{1,0:T(2,128)} %ex_hbm.1) | copy-start | bytes 52
  11.2 0.7 %copy-start.11 = (s32[64]{0:T(128)S(1)}, s32[64]{0:T(128)}, u32[]{:S(2)}) copy-start(s32[64]{0:T(128)} %param.17) | copy-start | bytes 772

commit v4 on v3

--- a/solution.py
+++ b/solution.py
@@ -8,12 +8,10 @@
 from jax.sharding import PartitionSpec as P
 
 MESH = pl.DeviceIdType.MESH
-VMEM = pl.BlockSpec(memory_space=pltpu.VMEM)
-HBM = pl.BlockSpec(memory_space=pltpu.HBM)
 ANY = pl.BlockSpec(memory_space=pl.ANY)
 SMEM = pl.BlockSpec(memory_space=pltpu.SMEM)
 step_ratio = 0.08
-limit = 24 * 1024 * 1024
+limit = 56 * 1024 * 1024
 sent = 6
 back = 4
 
@@ -88,12 +86,16 @@
     slots = dense.shape[1]
     position = lax.broadcasted_iota(jnp.int32, (n * cap, slots), 0)
     onehot = jnp.where(position == rank_row[...], 1.0, 0.0).astype(jnp.bfloat16)
-    for j in range(sent):
-        total = 0.0
-        for piece in split(dense[j], 3):
-            total = total + jnp.dot(onehot, piece, preferred_element_type=jnp.float32)
+    onehot = jnp.concatenate([onehot] * 3, 1)
+    width = dense.shape[2]
+    for j in range(0, sent, 2):
+        pair = [jnp.concatenate(split(dense[j + i], 3), 0) for i in range(2)]
+        total = jnp.dot(onehot, jnp.concatenate(pair, 1), preferred_element_type=jnp.float32)
         for s in range(n):
-            pay_ref[s, j * cap : (j + 1) * cap, :] = total[s * cap : (s + 1) * cap]
+            for i in range(2):
+                pay_ref[s, (j + i) * cap : (j + i + 1) * cap, :] = total[
+                    s * cap : (s + 1) * cap, i * width : (i + 1) * width
+                ]
 
 
 def face(a, b, ua, ub, wall):
@@ -123,9 +125,13 @@
     vox_hbm,
     lab_hbm,
     ex_hbm,
+    adv_out,
+    new_out,
+    ret_out,
+    calm_out,
+    pull_out,
     adv_ref,
     new_ref,
-    ret_ref,
     calm_ref,
     pull_ref,
     rho_ref,
@@ -153,6 +159,8 @@
     flux_z,
     picked,
     load_sem,
+    plane_sem,
+    store_sem,
     halo_send,
     halo_recv,
     pay_send,
@@ -189,79 +197,26 @@
         pltpu.make_async_copy(src, dst, load_sem.at[i])
         for i, (src, dst) in enumerate(
             (
-                (rho_hbm, rho_ref),
-                (vel_hbm, vel_ref),
-                (temp_hbm, temp_ref),
+                (rank_hbm, rank_row),
+                (map_hbm, map_ref),
+                (rank_hbm, rank_ref),
+                (count_hbm, count_ref),
+                (ex_hbm, ex_ref),
                 (mass_hbm, mass_ref),
                 (motion_hbm, motion_ref),
                 (kelvin_hbm, kelvin_ref),
                 (vox_hbm, vox_ref),
                 (lab_hbm, lab_ref),
-                (rank_hbm, rank_row),
-                (map_hbm, map_ref),
-                (rank_hbm, rank_ref),
-                (count_hbm, count_ref),
-                (ex_hbm, ex_ref),
+                (rho_hbm, rho_ref),
+                (vel_hbm, vel_ref),
+                (temp_hbm, temp_ref),
             )
         )
     ]
     for load in loads:
         load.start()
     lax.fori_loop(1, n, greet, 0)
-    for load in loads[:3]:
-        load.wait()
-
-    def prim(f, z, rows):
-        if f == 0:
-            return rho_ref[z, rows, :]
-        if f == 4:
-            return temp_ref[z, rows, :]
-        return vel_ref[f - 1, z, rows, :]
-
-    whole = pl.ds(0, height)
-    lanes = lax.broadcasted_iota(jnp.int32, (height, width), 1)
-
-    def pack(z, carry):
-        low, high = carry
-        for f in range(5):
-            spot = f * depth + z
-            x = prim(f, z, whole)
-            ysend[0, f, pl.ds(z, 1), :] = x[0:1]
-            ysend[1, f, pl.ds(z, 1), :] = x[height - 1 : height]
-            low = jnp.where(lanes == spot, pltpu.roll(x, spot, 1), low)
-            high = jnp.where(lanes == spot, pltpu.roll(x, spot + 1, 1), high)
-        return (low, high)
-
-    zero = jnp.zeros((height, width), jnp.float32)
-    low, high = lax.fori_loop(0, depth, pack, (zero, zero))
-    xsend[0] = low
-    xsend[1] = high
-    pl.semaphore_wait(barrier, n - 1)
-
-    def halo(which, side, device):
-        src, dst = ((xsend, xrecv), (ysend, yrecv))[which]
-        return pltpu.make_async_remote_copy(
-            src_ref=src.at[side],
-            dst_ref=dst.at[1 - side],
-            send_sem=halo_send.at[2 * which + side],
-            recv_sem=halo_recv.at[2 * which + 1 - side],
-            device_id=device,
-            device_id_type=MESH,
-        )
-
-    sides = (
-        (0, 0, gx > 0, (gx - 1, gy)),
-        (0, 1, gx < n_gx - 1, (gx + 1, gy)),
-        (1, 0, gy > 0, (gx, gy - 1)),
-        (1, 1, gy < n_gy - 1, (gx, gy + 1)),
-    )
-    for which, side, there, device in sides:
-
-        @pl.when(there)
-        def _(which=which, side=side, device=device):
-            halo(which, side, device).start()
-
-    for load in loads[3:]:
+    for load in loads[:10]:
         load.wait()
     bin_grains(
         rank_ref,
@@ -293,7 +248,70 @@
         outward(k).start()
         return carry
 
-    lax.fori_loop(1, n, send_out, 0)
+    pl.semaphore_wait(barrier, n - 1)
+    early = 1 + n // 4
+    lax.fori_loop(1, early, send_out, 0)
+    stores = [
+        pltpu.make_async_copy(src, dst, store_sem.at[i])
+        for i, (src, dst) in enumerate(
+            ((calm_ref, calm_out), (pull_ref, pull_out), (new_ref, new_out), (home, ret_out))
+        )
+    ]
+    for store in stores[:2]:
+        store.start()
+    for load in loads[10:]:
+        load.wait()
+
+    def prim(f, z, rows):
+        if f == 0:
+            return rho_ref[z, rows, :]
+        if f == 4:
+            return temp_ref[z, rows, :]
+        return vel_ref[f - 1, z, rows, :]
+
+    whole = pl.ds(0, height)
+    lanes = lax.broadcasted_iota(jnp.int32, (height, width), 1)
+
+    def pack(z, carry):
+        low, high = carry
+        for f in range(5):
+            spot = f * depth + z
+            x = prim(f, z, whole)
+            ysend[0, f, pl.ds(z, 1), :] = x[0:1]
+            ysend[1, f, pl.ds(z, 1), :] = x[height - 1 : height]
+            low = jnp.where(lanes == spot, pltpu.roll(x, spot, 1), low)
+            high = jnp.where(lanes == spot, pltpu.roll(x, spot + 1, 1), high)
+        return (low, high)
+
+    zero = jnp.zeros((height, width), jnp.float32)
+    low, high = lax.fori_loop(0, depth, pack, (zero, zero))
+    xsend[0] = low
+    xsend[1] = high
+
+    def halo(which, side, device):
+        src, dst = ((xsend, xrecv), (ysend, yrecv))[which]
+        return pltpu.make_async_remote_copy(
+            src_ref=src.at[side],
+            dst_ref=dst.at[1 - side],
+            send_sem=halo_send.at[2 * which + side],
+            recv_sem=halo_recv.at[2 * which + 1 - side],
+            device_id=device,
+            device_id_type=MESH,
+        )
+
+    sides = (
+        (0, 0, gx > 0, (gx - 1, gy)),
+        (0, 1, gx < n_gx - 1, (gx + 1, gy)),
+        (1, 0, gy > 0, (gx, gy - 1)),
+        (1, 1, gy < n_gy - 1, (gx, gy + 1)),
+    )
+    for which, side, there, device in sides:
+
+        @pl.when(there)
+        def _(which=which, side=side, device=device):
+            halo(which, side, device).start()
+
+    lax.fori_loop(early, n, send_out, 0)
 
     for which, side, there, device in sides:
         recv = (xrecv, yrecv)[which]
@@ -324,6 +342,12 @@
     first, last = lane == 0, lane == width - 1
     wall_low = jnp.logical_and(first, west)
     wall_high = jnp.logical_and(last, east)
+
+    def plane_out(z):
+        rows = pl.ds(z * height, height)
+        return pltpu.make_async_copy(
+            adv_ref.at[:, rows, :], adv_out.at[:, rows, :], plane_sem.at[z]
+        )
 
     def plane(z, carry):
         above = jnp.minimum(z + 1, depth - 1)
@@ -386,6 +410,7 @@
             adv_ref[0, out, :] = fresh[0]
             for f in range(1, 5):
                 adv_ref[f, out, :] = fresh[f] * scale
+        plane_out(z).start()
         return carry
 
     lax.fori_loop(0, depth, plane, 0)
@@ -436,29 +461,80 @@
 
     lax.fori_loop(1, n, answer, 0)
 
+    stores[2].start()
+
     def finish(k, carry):
         inward(k).wait()
         return carry
 
     lax.fori_loop(1, n, finish, 0)
-    ret_ref[...] = home[...]
+    stores[3].start()
+    for store in stores:
+        store.wait()
+    for z in range(depth):
+        plane_out(z).wait()
 
 
 def final_kernel(
-    cap, rank_ref, map_ref, adv_ref, new_ref, ret_ref, calm_ref, pull_ref, out_ref, solid_ref, held, sem
+    cap,
+    rank_ref,
+    map_ref,
+    adv_ref,
+    new_hbm,
+    ret_hbm,
+    calm_hbm,
+    pull_hbm,
+    out_ref,
+    solid_out,
+    held,
+    new_ref,
+    ret_ref,
+    calm_ref,
+    pull_ref,
+    solid_ref,
+    load_sem,
+    store_sem,
 ):
     slots = rank_ref.shape[0]
     positions = map_ref.shape[1]
     fields, blocks, width = adv_ref.shape
 
-    def whole(f, inward):
-        here = held.at[f, pl.ds(0, blocks), :]
-        if inward:
-            return pltpu.make_async_copy(adv_ref.at[f], here, sem.at[f])
-        return pltpu.make_async_copy(here, out_ref.at[f], sem.at[f])
-
-    for f in range(fields):
-        whole(f, True).start()
+    def rows(f):
+        return held.at[f, pl.ds(0, blocks), :]
+
+    loads = [
+        pltpu.make_async_copy(src, dst, load_sem.at[i])
+        for i, (src, dst) in enumerate(
+            [(new_hbm, new_ref)]
+            + [(adv_ref.at[f], rows(f)) for f in range(fields)]
+            + [(ret_hbm, ret_ref), (calm_hbm, calm_ref), (pull_hbm, pull_ref)]
+        )
+    ]
+    stores = [
+        pltpu.make_async_copy(src, dst, store_sem.at[i])
+        for i, (src, dst) in enumerate(
+            [(rows(f), out_ref.at[f]) for f in range(fields)] + [(solid_ref, solid_out)]
+        )
+    ]
+    for load in loads:
+        load.start()
+    for load in loads[: fields + 1]:
+        load.wait()
+    stores[0].start()
+
+    def scatter(i, carry):
+        for u in range(cap):
+            b = map_ref[0, i * cap + u]
+            b = jnp.where(b >= 0, b, blocks)
+            for j in range(back):
+                held[1 + j, pl.ds(b, 1), :] = new_ref[i, j * cap + u : j * cap + u + 1, :]
+        return carry
+
+    lax.fori_loop(0, positions // cap, scatter, 0)
+    for f in range(1, fields):
+        stores[f].start()
+    for load in loads[fields + 1 :]:
+        load.wait()
     unroll = 8
 
     def solid(i, carry):
@@ -475,23 +551,9 @@
     lax.fori_loop(0, slots // unroll, solid, 0)
     for j in range(back):
         solid_ref[j] = calm_ref[j] + pull_ref[j // 3] * solid_ref[j]
-    for f in range(fields):
-        whole(f, True).wait()
-    whole(0, False).start()
-
-    def scatter(i, carry):
-        for u in range(cap):
-            b = map_ref[0, i * cap + u]
-            b = jnp.where(b >= 0, b, blocks)
-            for j in range(back):
-                held[1 + j, pl.ds(b, 1), :] = new_ref[i, j * cap + u : j * cap + u + 1, :]
-        return carry
-
-    lax.fori_loop(0, positions // cap, scatter, 0)
-    for f in range(1, fields):
-        whole(f, False).start()
-    for f in range(fields):
-        whole(f, False).wait()
+    stores[fields].start()
+    for store in stores:
+        store.wait()
 
 
 def per_device(
@@ -527,9 +589,13 @@
             shape((back, 2 * slots, width), f32),
             shape((2, 2 * slots, width), f32),
         ),
-        in_specs=[HBM] * 12,
-        out_specs=(VMEM,) * 5,
+        in_specs=[ANY] * 12,
+        out_specs=(ANY,) * 5,
         scratch_shapes=[
+            pltpu.VMEM((5, blocks, width), f32),
+            pltpu.VMEM((n, back * cap, width), f32),
+            pltpu.VMEM((back, 2 * slots, width), f32),
+            pltpu.VMEM((2, 2 * slots, width), f32),
             pltpu.VMEM((depth, height, width), f32),
             pltpu.VMEM((3, depth, height, width), f32),
             pltpu.VMEM((depth, height, width), f32),
@@ -555,6 +621,8 @@
             pltpu.VMEM((5, height, width), f32),
             pltpu.VMEM((n, 5 * cap, width), f32),
             dma((13,)),
+            dma((depth,)),
+            dma((4,)),
             dma((4,)),
             dma((4,)),
             dma((n,)),
@@ -583,9 +651,18 @@
     final, solid = pl.pallas_call(
         functools.partial(final_kernel, cap),
         out_shape=(shape((5, blocks, width), f32), shape((back, 2 * slots, width), f32)),
-        in_specs=[SMEM] * 2 + [ANY] + [VMEM] * 4,
-        out_specs=(ANY, VMEM),
-        scratch_shapes=[pltpu.VMEM((5, blocks + 8, width), f32), dma((5,))],
+        in_specs=[SMEM] * 2 + [ANY] * 5,
+        out_specs=(ANY, ANY),
+        scratch_shapes=[
+            pltpu.VMEM((5, blocks + 8, width), f32),
+            pltpu.VMEM((n, back * cap, width), f32),
+            pltpu.VMEM((n, back * cap, width), f32),
+            pltpu.VMEM((back, 2 * slots, width), f32),
+            pltpu.VMEM((2, 2 * slots, width), f32),
+            pltpu.VMEM((back, 2 * slots, width), f32),
+            dma((9,)),
+            dma((6,)),
+        ],
         compiler_params=pltpu.CompilerParams(vmem_limit_bytes=limit),
         name="place_results",
     )(receiver_arrival_rank, sender_tile_map, adv, new, ret, calm, pull)

time: 61.3 us -> 49.2 us (0.80)
  local copies, waits for them, and re-layouts: 11.2 us -> 0 us
    unnamed x24 -> x0, local copies, waits for them, and re-layouts: 11.2 us -> none
    pallas_call x1, Pallas kernels: 44.8 us -> 43 us  [per_device(): pl.pallas_call(functools.partial(grid_kernel, n_gx, n_gy), out_shape=(sha...]
    pallas_call x1, Pallas kernels: 4.18 us -> 5.44 us  [per_device(): pl.pallas_call(functools.partial(final_kernel, cap), out_shape=(shape((5,...]
where the time goes in v4:
time: 49.2 us; the launch traced here: 49.1 us
  Pallas kernels  48.4 us (98%)
  between operations  0.64 us (1%)
    pallas_call x1, Pallas kernels, per_device(): pl.pallas_call(functools.partial(grid_kernel, n_gx, n_gy), out_shape=(sha...  43 us
    pallas_call x1, Pallas kernels, per_device(): pl.pallas_call(functools.partial(final_kernel, cap), out_shape=(shape((5,...  5.44 us

profile of v4, /device:TPU:0, one launch (start us, length us, event | category | flops | bytes accessed | tf_op | source)
XLA Modules:
  0.0 49.1 jit_solution(4288675411776359425)
XLA Ops:
  0.6 43.0 %advance_and_couple.1 = (f32[5,1536,128]{2,1,0:T(8,128)}, f32[32,32,128]{2,1,0:T(8,128)}, f32[32,32,128]{2,1,0:T(8,128)}, f32[4,128,128]{2,1,0:T(8,128)}, f32[2,128,128]{2,1,0:T(8,128)}) custom-call(f32[16,96,128]{2,1,0:T(8,128)} %rho_hbm.1, f32[3,16,96,128]{3,2,1,0:T(8,128)} %vel_hbm.1, f32[16,96,128]{2,1,0:T(8,128)} %temp_hbm.1, s32[1,256]{1,0:T(1,128)} %map_ref.1, ...), custom_call_target="tpu_custom_call" | custom-call | tf_op jit(solution)/shard_map/advance_and_couple/pallas_call | solution.py:583
  43.6 5.4 %place_results.1 = (f32[5,1536,128]{2,1,0:T(8,128)}, f32[4,128,128]{2,1,0:T(8,128)}) custom-call(s32[64]{0:T(128)} %rank_ref.1, s32[1,256]{1,0:T(1,128)} %map_ref.1, f32[5,1536,128]{2,1,0:T(8,128)} %get-tuple-element.9.adv_ref, f32[32,32,128]{2,1,0:T(8,128)} %get-tuple-element.10.new_hbm, f32[32,32,128]{2,1,0:T(8,128)} %get-tuple-element.11.ret_hbm, ...), custom_call_target="tpu_custom_call" | custom-call | tf_op jit(solution)/shard_map/place_results/pallas_call | solution.py:651

commit v5 on v4

--- a/solution.py
+++ b/solution.py
@@ -126,11 +126,13 @@
     lab_hbm,
     ex_hbm,
     adv_out,
-    new_out,
     ret_out,
     calm_out,
     pull_out,
     adv_ref,
+    fin_ref,
+    index_row,
+    index_ref,
     new_ref,
     calm_ref,
     pull_ref,
@@ -160,6 +162,8 @@
     picked,
     load_sem,
     plane_sem,
+    final_sem,
+    index_sem,
     store_sem,
     halo_send,
     halo_recv,
@@ -254,7 +258,7 @@
     stores = [
         pltpu.make_async_copy(src, dst, store_sem.at[i])
         for i, (src, dst) in enumerate(
-            ((calm_ref, calm_out), (pull_ref, pull_out), (new_ref, new_out), (home, ret_out))
+            ((calm_ref, calm_out), (pull_ref, pull_out), (home, ret_out))
         )
     ]
     for store in stores[:2]:
@@ -312,6 +316,20 @@
             halo(which, side, device).start()
 
     lax.fori_loop(early, n, send_out, 0)
+
+    blocks = depth * height
+    number = lax.broadcasted_iota(jnp.int32, index_row.shape, 0) * width
+    number = number + lax.broadcasted_iota(jnp.int32, index_row.shape, 1)
+
+    def mark(s, index):
+        for r in range(cap):
+            i = s * cap + r
+            index = jnp.where(number == map_ref[0, i], blocks + i, index)
+        return index
+
+    index_row[...] = lax.fori_loop(0, n, mark, number)
+    index_copy = pltpu.make_async_copy(index_row, index_ref, index_sem)
+    index_copy.start()
 
     for which, side, there, device in sides:
         recv = (xrecv, yrecv)[which]
@@ -346,7 +364,13 @@
     def plane_out(z):
         rows = pl.ds(z * height, height)
         return pltpu.make_async_copy(
-            adv_ref.at[:, rows, :], adv_out.at[:, rows, :], plane_sem.at[z]
+            adv_ref.at[0, rows, :], adv_out.at[0, rows, :], plane_sem.at[z]
+        )
+
+    def final_out(z):
+        rows = pl.ds(z * height, height)
+        return pltpu.make_async_copy(
+            fin_ref.at[:, rows, :], adv_out.at[pl.ds(1, back), rows, :], final_sem.at[z]
         )
 
     def plane(z, carry):
@@ -430,13 +454,11 @@
     def couple(ref, s):
         g = part(picked, s, 0)
         scale = 1.0 / (g + part(ref, s, 0))
-        for c in range(3):
-            new_ref[s, c * cap : (c + 1) * cap, :] = (
-                g * part(picked, s, 1 + c) + part(ref, s, 1 + c)
-            ) * scale
-        new_ref[s, 3 * cap : 4 * cap, :] = (g * part(picked, s, 4) + part(ref, s, 4)) / (
-            g + part(ref, s, 5)
-        )
+        fresh = [(g * part(picked, s, 1 + c) + part(ref, s, 1 + c)) * scale for c in range(3)]
+        fresh.append((g * part(picked, s, 4) + part(ref, s, 4)) / (g + part(ref, s, 5)))
+        for j in range(back):
+            new_ref[s, j * cap : (j + 1) * cap, :] = fresh[j]
+            adv_ref[1 + j, pl.ds(blocks + s * cap, cap), :] = fresh[j]
 
     couple(pay_ref, me)
     home[me] = new_ref[me]
@@ -461,33 +483,46 @@
 
     lax.fori_loop(1, n, answer, 0)
 
-    stores[2].start()
+    index_copy.wait()
+    unroll = 8
+
+    def assemble(z, carry):
+        def some(i, carry):
+            for u in range(unroll):
+                b = z * height + i * unroll + u
+                source = index_ref[b // width, lax.rem(b, width)]
+                for j in range(back):
+                    fin_ref[j, pl.ds(b, 1), :] = adv_ref[1 + j, pl.ds(source, 1), :]
+            return carry
+
+        lax.fori_loop(0, height // unroll, some, 0)
+        final_out(z).start()
+        return carry
+
+    lax.fori_loop(0, depth, assemble, 0)
 
     def finish(k, carry):
         inward(k).wait()
         return carry
 
     lax.fori_loop(1, n, finish, 0)
-    stores[3].start()
+    stores[2].start()
     for store in stores:
         store.wait()
     for z in range(depth):
         plane_out(z).wait()
+        final_out(z).wait()
 
 
 def final_kernel(
     cap,
     rank_ref,
-    map_ref,
     adv_ref,
-    new_hbm,
     ret_hbm,
     calm_hbm,
     pull_hbm,
     out_ref,
     solid_out,
-    held,
-    new_ref,
     ret_ref,
     calm_ref,
     pull_ref,
@@ -496,44 +531,24 @@
     store_sem,
 ):
     slots = rank_ref.shape[0]
-    positions = map_ref.shape[1]
     fields, blocks, width = adv_ref.shape
-
-    def rows(f):
-        return held.at[f, pl.ds(0, blocks), :]
-
     loads = [
         pltpu.make_async_copy(src, dst, load_sem.at[i])
         for i, (src, dst) in enumerate(
-            [(new_hbm, new_ref)]
-            + [(adv_ref.at[f], rows(f)) for f in range(fields)]
-            + [(ret_hbm, ret_ref), (calm_hbm, calm_ref), (pull_hbm, pull_ref)]
+            ((ret_hbm, ret_ref), (calm_hbm, calm_ref), (pull_hbm, pull_ref))
         )
     ]
     stores = [
         pltpu.make_async_copy(src, dst, store_sem.at[i])
         for i, (src, dst) in enumerate(
-            [(rows(f), out_ref.at[f]) for f in range(fields)] + [(solid_ref, solid_out)]
+            [(adv_ref.at[f], out_ref.at[f]) for f in range(fields)] + [(solid_ref, solid_out)]
         )
     ]
     for load in loads:
         load.start()
-    for load in loads[: fields + 1]:
-        load.wait()
-    stores[0].start()
-
-    def scatter(i, carry):
-        for u in range(cap):
-            b = map_ref[0, i * cap + u]
-            b = jnp.where(b >= 0, b, blocks)
-            for j in range(back):
-                held[1 + j, pl.ds(b, 1), :] = new_ref[i, j * cap + u : j * cap + u + 1, :]
-        return carry
-
-    lax.fori_loop(0, positions // cap, scatter, 0)
-    for f in range(1, fields):
-        stores[f].start()
-    for load in loads[fields + 1 :]:
+    for store in stores[:fields]:
+        store.start()
+    for load in loads:
         load.wait()
     unroll = 8
 
@@ -580,19 +595,21 @@
     f32, i32 = jnp.float32, jnp.int32
     shape = jax.ShapeDtypeStruct
     dma = pltpu.SemaphoreType.DMA
-    adv, new, ret, calm, pull = pl.pallas_call(
+    adv, ret, calm, pull = pl.pallas_call(
         functools.partial(grid_kernel, n_gx, n_gy),
         out_shape=(
             shape((5, blocks, width), f32),
-            shape((n, back * cap, width), f32),
             shape((n, back * cap, width), f32),
             shape((back, 2 * slots, width), f32),
             shape((2, 2 * slots, width), f32),
         ),
         in_specs=[ANY] * 12,
-        out_specs=(ANY,) * 5,
+        out_specs=(ANY,) * 4,
         scratch_shapes=[
-            pltpu.VMEM((5, blocks, width), f32),
+            pltpu.VMEM((5, blocks + n * cap, width), f32),
+            pltpu.VMEM((back, blocks, width), f32),
+            pltpu.VMEM((blocks // width, width), i32),
+            pltpu.SMEM((blocks // width, width), i32),
             pltpu.VMEM((n, back * cap, width), f32),
             pltpu.VMEM((back, 2 * slots, width), f32),
             pltpu.VMEM((2, 2 * slots, width), f32),
@@ -622,7 +639,9 @@
             pltpu.VMEM((n, 5 * cap, width), f32),
             dma((13,)),
             dma((depth,)),
-            dma((4,)),
+            dma((depth,)),
+            dma,
+            dma((3,)),
             dma((4,)),
             dma((4,)),
             dma((n,)),
@@ -651,21 +670,19 @@
     final, solid = pl.pallas_call(
         functools.partial(final_kernel, cap),
         out_shape=(shape((5, blocks, width), f32), shape((back, 2 * slots, width), f32)),
-        in_specs=[SMEM] * 2 + [ANY] * 5,
+        in_specs=[SMEM] + [ANY] * 4,
         out_specs=(ANY, ANY),
         scratch_shapes=[
-            pltpu.VMEM((5, blocks + 8, width), f32),
-            pltpu.VMEM((n, back * cap, width), f32),
             pltpu.VMEM((n, back * cap, width), f32),
             pltpu.VMEM((back, 2 * slots, width), f32),
             pltpu.VMEM((2, 2 * slots, width), f32),
             pltpu.VMEM((back, 2 * slots, width), f32),
-            dma((9,)),
+            dma((3,)),
             dma((6,)),
         ],
         compiler_params=pltpu.CompilerParams(vmem_limit_bytes=limit),
         name="place_results",
-    )(receiver_arrival_rank, sender_tile_map, adv, new, ret, calm, pull)
+    )(receiver_arrival_rank, adv, ret, calm, pull)
     return (
         final.reshape(5, depth, height, width),
         solid.reshape(back, slots, 2, width),

time: 49.2 us -> 168 us (3.41)
  the two profiles are of different devices: /device:TPU:0 before, /device:TPU:5 now
where the time goes in v5:
time: 168 us
  Pallas kernels  167 us (99%)
    pallas_call x1, Pallas kernels, per_device(): pl.pallas_call(functools.partial(final_kernel, cap), out_shape=(shape((5,...  121 us
    pallas_call x1, Pallas kernels, per_device(): pl.pallas_call(functools.partial(grid_kernel, n_gx, n_gy), out_shape=(sha...  46.4 us

profile of v5, /device:TPU:5, one launch (start us, length us, event | category | flops | bytes accessed | tf_op | source)
XLA Modules:
  0.0 168.0 jit_solution(8379318874564086609)
XLA Ops:
  0.6 46.4 %advance_and_couple.1 = (f32[5,1536,128]{2,1,0:T(8,128)}, f32[32,32,128]{2,1,0:T(8,128)}, f32[4,128,128]{2,1,0:T(8,128)}, f32[2,128,128]{2,1,0:T(8,128)}) custom-call(f32[16,96,128]{2,1,0:T(8,128)} %rho_hbm.1, f32[3,16,96,128]{3,2,1,0:T(8,128)} %vel_hbm.1, f32[16,96,128]{2,1,0:T(8,128)} %temp_hbm.1, s32[1,256]{1,0:T(1,128)} %map_hbm.1, s32[1,64]{1,0:T(1,128)} %bitcast.4, ...), custom_call_target="tpu_custom_call" | custom-call | tf_op jit(solution)/shard_map/advance_and_couple/pallas_call | solution.py:598
  47.1 121.0 %place_results.1 = (f32[5,1536,128]{2,1,0:T(8,128)}, f32[4,128,128]{2,1,0:T(8,128)}) custom-call(s32[64]{0:T(128)} %rank_ref.1, f32[5,1536,128]{2,1,0:T(8,128)} %get-tuple-element.8.adv_ref, f32[32,32,128]{2,1,0:T(8,128)} %get-tuple-element.9.ret_hbm, f32[4,128,128]{2,1,0:T(8,128)} %get-tuple-element.10.calm_hbm, f32[2,128,128]{2,1,0:T(8,128)} %get-tuple-element.11.pull_hbm), custom_call_target="tpu_custom_call" | custom-call | tf_op jit(solution)/shard_map/place_results/pallas_call | solution.py:670

commit v6 on v5

--- a/solution.py
+++ b/solution.py
@@ -440,10 +440,10 @@
     lax.fori_loop(0, depth, plane, 0)
 
     def pick(s, carry):
-        for r in range(cap):
-            b = jnp.maximum(map_ref[0, s * cap + r], 0)
-            for f in range(5):
-                picked[s, f * cap + r : f * cap + r + 1, :] = adv_ref[f, pl.ds(b, 1), :]
+        at = [jnp.maximum(map_ref[0, s * cap + r], 0) for r in range(cap)]
+        for f in range(5):
+            found = [adv_ref[f, pl.ds(b, 1), :] for b in at]
+            picked[s, f * cap : (f + 1) * cap, :] = jnp.concatenate(found, 0)
         return carry
 
     lax.fori_loop(0, n, pick, 0)
@@ -488,11 +488,11 @@
 
     def assemble(z, carry):
         def some(i, carry):
-            for u in range(unroll):
-                b = z * height + i * unroll + u
-                source = index_ref[b // width, lax.rem(b, width)]
-                for j in range(back):
-                    fin_ref[j, pl.ds(b, 1), :] = adv_ref[1 + j, pl.ds(source, 1), :]
+            b = z * height + i * unroll
+            at = [index_ref[b // width, lax.rem(b, width) + u] for u in range(unroll)]
+            for j in range(back):
+                found = [adv_ref[1 + j, pl.ds(source, 1), :] for source in at]
+                fin_ref[j, pl.ds(b, unroll), :] = jnp.concatenate(found, 0)
             return carry
 
         lax.fori_loop(0, height // unroll, some, 0)
@@ -523,6 +523,7 @@
     pull_hbm,
     out_ref,
     solid_out,
+    held,
     ret_ref,
     calm_ref,
     pull_ref,
@@ -535,21 +536,23 @@
     loads = [
         pltpu.make_async_copy(src, dst, load_sem.at[i])
         for i, (src, dst) in enumerate(
-            ((ret_hbm, ret_ref), (calm_hbm, calm_ref), (pull_hbm, pull_ref))
+            [(ret_hbm, ret_ref), (calm_hbm, calm_ref), (pull_hbm, pull_ref)]
+            + [(adv_ref.at[f], held.at[f]) for f in range(fields)]
         )
     ]
     stores = [
         pltpu.make_async_copy(src, dst, store_sem.at[i])
         for i, (src, dst) in enumerate(
-            [(adv_ref.at[f], out_ref.at[f]) for f in range(fields)] + [(solid_ref, solid_out)]
+            [(held.at[f], out_ref.at[f]) for f in range(fields)] + [(solid_ref, solid_out)]
         )
     ]
     for load in loads:
         load.start()
-    for store in stores[:fields]:
-        store.start()
-    for load in loads:
+    for load in loads[:3]:
         load.wait()
+    for f in range(2):
+        loads[3 + f].wait()
+        stores[f].start()
     unroll = 8
 
     def solid(i, carry):
@@ -558,14 +561,17 @@
             v = jnp.maximum(rank_ref[k], 0)
             s = v // cap
             r = v % cap
+            rows = [ret_ref[s, pl.ds(j * cap + r, 1), :] for j in range(back)]
             for j in range(back):
-                row = ret_ref[s, pl.ds(j * cap + r, 1), :]
-                solid_ref[j, pl.ds(2 * k, 2), :] = jnp.broadcast_to(row, (2, width))
+                solid_ref[j, pl.ds(2 * k, 2), :] = jnp.broadcast_to(rows[j], (2, width))
         return carry
 
     lax.fori_loop(0, slots // unroll, solid, 0)
     for j in range(back):
         solid_ref[j] = calm_ref[j] + pull_ref[j // 3] * solid_ref[j]
+    for f in range(2, fields):
+        loads[3 + f].wait()
+        stores[f].start()
     stores[fields].start()
     for store in stores:
         store.wait()
@@ -673,11 +679,12 @@
         in_specs=[SMEM] + [ANY] * 4,
         out_specs=(ANY, ANY),
         scratch_shapes=[
+            pltpu.VMEM((5, blocks, width), f32),
             pltpu.VMEM((n, back * cap, width), f32),
             pltpu.VMEM((back, 2 * slots, width), f32),
             pltpu.VMEM((2, 2 * slots, width), f32),
             pltpu.VMEM((back, 2 * slots, width), f32),
-            dma((3,)),
+            dma((8,)),
             dma((6,)),
         ],
         compiler_params=pltpu.CompilerParams(vmem_limit_bytes=limit),

time: 168 us -> 48.2 us (0.29)
  the two profiles are of different devices: /device:TPU:5 before, /device:TPU:0 now
where the time goes in v6:
time: 48.2 us; the launch traced here: 48.1 us
  Pallas kernels  47.4 us (98%)
  between operations  0.64 us (1%)
    pallas_call x1, Pallas kernels, per_device(): pl.pallas_call(functools.partial(grid_kernel, n_gx, n_gy), out_shape=(sha...  43.2 us
    pallas_call x1, Pallas kernels, per_device(): pl.pallas_call(functools.partial(final_kernel, cap), out_shape=(shape((5,...  4.26 us

profile of v6, /device:TPU:0, one launch (start us, length us, event | category | flops | bytes accessed | tf_op | source)
XLA Modules:
  0.0 48.1 jit_solution(16021563430586247720)
XLA Ops:
  0.6 43.2 %advance_and_couple.1 = (f32[5,1536,128]{2,1,0:T(8,128)}, f32[32,32,128]{2,1,0:T(8,128)}, f32[4,128,128]{2,1,0:T(8,128)}, f32[2,128,128]{2,1,0:T(8,128)}) custom-call(f32[16,96,128]{2,1,0:T(8,128)} %rho_hbm.1, f32[3,16,96,128]{3,2,1,0:T(8,128)} %vel_hbm.1, f32[16,96,128]{2,1,0:T(8,128)} %temp_hbm.1, s32[1,256]{1,0:T(1,128)} %map_hbm.1, s32[1,64]{1,0:T(1,128)} %bitcast.4, ...), custom_call_target="tpu_custom_call" | custom-call | tf_op jit(solution)/shard_map/advance_and_couple/pallas_call | solution.py:604
  43.8 4.3 %place_results.1 = (f32[5,1536,128]{2,1,0:T(8,128)}, f32[4,128,128]{2,1,0:T(8,128)}) custom-call(s32[64]{0:T(128)} %rank_ref.1, f32[5,1536,128]{2,1,0:T(8,128)} %get-tuple-element.8.adv_ref, f32[32,32,128]{2,1,0:T(8,128)} %get-tuple-element.9.ret_hbm, f32[4,128,128]{2,1,0:T(8,128)} %get-tuple-element.10.calm_hbm, f32[2,128,128]{2,1,0:T(8,128)} %get-tuple-element.11.pull_hbm), custom_call_target="tpu_custom_call" | custom-call | tf_op jit(solution)/shard_map/place_results/pallas_call | solution.py:676

commit v7 on v6

--- a/solution.py
+++ b/solution.py
@@ -98,8 +98,13 @@
                 ]
 
 
+def inverse(x):
+    near = pl.reciprocal(x, approx=True)
+    return near * (2.0 - x * near)
+
+
 def face(a, b, ua, ub, wall):
-    speed = 0.5 * (ua + ub) - (2.0 * step_ratio) * (b[4] - a[4]) / (a[0] + b[0])
+    speed = 0.5 * (ua + ub) - (2.0 * step_ratio) * (b[4] - a[4]) * inverse(a[0] + b[0])
     speed = jnp.where(wall, 0.0, speed)
     ahead = speed > 0
     return [speed * jnp.where(ahead, x, y) for x, y in zip(a, b)]
@@ -159,6 +164,7 @@
     home,
     ext,
     flux_z,
+    edge_x,
     picked,
     load_sem,
     plane_sem,
@@ -318,19 +324,6 @@
     lax.fori_loop(early, n, send_out, 0)
 
     blocks = depth * height
-    number = lax.broadcasted_iota(jnp.int32, index_row.shape, 0) * width
-    number = number + lax.broadcasted_iota(jnp.int32, index_row.shape, 1)
-
-    def mark(s, index):
-        for r in range(cap):
-            i = s * cap + r
-            index = jnp.where(number == map_ref[0, i], blocks + i, index)
-        return index
-
-    index_row[...] = lax.fori_loop(0, n, mark, number)
-    index_copy = pltpu.make_async_copy(index_row, index_ref, index_sem)
-    index_copy.start()
-
     for which, side, there, device in sides:
         recv = (xrecv, yrecv)[which]
 
@@ -359,7 +352,15 @@
     row = lax.broadcasted_iota(jnp.int32, (chunk + 8, width), 0)
     first, last = lane == 0, lane == width - 1
     wall_low = jnp.logical_and(first, west)
-    wall_high = jnp.logical_and(last, east)
+
+    def lined(ref):
+        packed = ref[1]
+        return [packed] + [pltpu.roll(packed, width - f * depth, 1) for f in range(1, 5)]
+
+    inner, beyond = lined(xsend), lined(xrecv)
+    rim = face(conserve(inner), conserve(beyond), inner[1], beyond[1], east)
+    for f in range(5):
+        edge_x[f] = rim[f]
 
     def plane_out(z):
         rows = pl.ds(z * height, height)
@@ -405,7 +406,7 @@
             flux = face(lower[:5], upper[:5], lower[5], upper[5], wall)
             for f in range(5):
                 change[f] = change[f] + (flux[f][1 : chunk + 1] - flux[f][:chunk])
-            left, right = [], []
+            left = []
             for f in range(5):
                 spot = f * depth + z
                 left.append(
@@ -415,21 +416,16 @@
                         pltpu.roll(own[f], 1, 1),
                     )
                 )
-                right.append(
-                    jnp.where(
-                        last,
-                        pltpu.roll(xrecv[1, rows, :], width - 1 - spot, 1),
-                        pltpu.roll(own[f], width - 1, 1),
-                    )
-                )
             flux = face(conserve(left), cons, left[1], own[1], wall_low)
             for f in range(5):
-                change[f] = change[f] - flux[f]
-            flux = face(cons, conserve(right), own[1], right[1], wall_high)
-            for f in range(5):
-                change[f] = change[f] + flux[f]
+                over = jnp.where(
+                    last,
+                    pltpu.roll(edge_x[f, rows, :], width - 1 - z, 1),
+                    pltpu.roll(flux[f], width - 1, 1),
+                )
+                change[f] = change[f] + (over - flux[f])
             fresh = [cons[f] - step_ratio * change[f] for f in range(5)]
-            scale = 1.0 / fresh[0]
+            scale = inverse(fresh[0])
             out = pl.ds(z * height + y0, chunk)
             adv_ref[0, out, :] = fresh[0]
             for f in range(1, 5):
@@ -482,6 +478,19 @@
         return carry
 
     lax.fori_loop(1, n, answer, 0)
+
+    number = lax.broadcasted_iota(jnp.int32, index_row.shape, 0) * width
+    number = number + lax.broadcasted_iota(jnp.int32, index_row.shape, 1)
+
+    def mark(s, index):
+        for r in range(cap):
+            i = s * cap + r
+            index = jnp.where(number == map_ref[0, i], blocks + i, index)
+        return index
+
+    index_row[...] = lax.fori_loop(0, n, mark, number)
+    index_copy = pltpu.make_async_copy(index_row, index_ref, index_sem)
+    index_copy.start()
 
     index_copy.wait()
     unroll = 8
@@ -642,6 +651,7 @@
             pltpu.VMEM((n, back * cap, width), f32),
             pltpu.VMEM((6, height + 16, width), f32),
             pltpu.VMEM((5, height, width), f32),
+            pltpu.VMEM((5, height, width), f32),
             pltpu.VMEM((n, 5 * cap, width), f32),
             dma((13,)),
             dma((depth,)),

time: 48.2 us -> 48.2 us (level)
  no operation moved by 1% of the time
where the time goes in v7:
time: 48.2 us; the launch traced here: 48.1 us
  Pallas kernels  47.4 us (98%)
  between operations  0.64 us (1%)
    pallas_call x1, Pallas kernels, per_device(): pl.pallas_call(functools.partial(grid_kernel, n_gx, n_gy), out_shape=(sha...  43.2 us
    pallas_call x1, Pallas kernels, per_device(): pl.pallas_call(functools.partial(final_kernel, cap), out_shape=(shape((5,...  4.26 us

profile of v7, /device:TPU:0, one launch (start us, length us, event | category | flops | bytes accessed | tf_op | source)
XLA Modules:
  0.0 48.1 jit_solution(13855304611837797177)
XLA Ops:
  0.6 43.2 %advance_and_couple.1 = (f32[5,1536,128]{2,1,0:T(8,128)}, f32[32,32,128]{2,1,0:T(8,128)}, f32[4,128,128]{2,1,0:T(8,128)}, f32[2,128,128]{2,1,0:T(8,128)}) custom-call(f32[16,96,128]{2,1,0:T(8,128)} %rho_hbm.1, f32[3,16,96,128]{3,2,1,0:T(8,128)} %vel_hbm.1, f32[16,96,128]{2,1,0:T(8,128)} %temp_hbm.1, s32[1,256]{1,0:T(1,128)} %map_hbm.1, s32[1,64]{1,0:T(1,128)} %bitcast.4, ...), custom_call_target="tpu_custom_call" | custom-call | tf_op jit(solution)/shard_map/advance_and_couple/pallas_call | solution.py:613
  43.8 4.3 %place_results.1 = (f32[5,1536,128]{2,1,0:T(8,128)}, f32[4,128,128]{2,1,0:T(8,128)}) custom-call(s32[64]{0:T(128)} %rank_ref.1, f32[5,1536,128]{2,1,0:T(8,128)} %get-tuple-element.8.adv_ref, f32[32,32,128]{2,1,0:T(8,128)} %get-tuple-element.9.ret_hbm, f32[4,128,128]{2,1,0:T(8,128)} %get-tuple-element.10.calm_hbm, f32[2,128,128]{2,1,0:T(8,128)} %get-tuple-element.11.pull_hbm), custom_call_target="tpu_custom_call" | custom-call | tf_op jit(solution)/shard_map/place_results/pallas_call | solution.py:686

commit v8 on v7

--- a/solution.py
+++ b/solution.py
@@ -47,11 +47,11 @@
             )
             onehot = jnp.where(cells == vox_ref[here, :], 1.0, 0.0).astype(jnp.bfloat16)
             total = lax.dot_general(
+                onehot,
                 jnp.concatenate(split(values, 2), 0),
-                onehot,
                 (((1,), (1,)), ((), ())),
                 preferred_element_type=jnp.float32,
-            )
+            ).T
             total = total[:16] + total[16:]
             pay = 0.0
             live = jnp.where(rank_ref[0, k] >= 0, 1.0, 0.0)
@@ -575,12 +575,14 @@
                 solid_ref[j, pl.ds(2 * k, 2), :] = jnp.broadcast_to(rows[j], (2, width))
         return carry
 
-    lax.fori_loop(0, slots // unroll, solid, 0)
+    steps = slots // unroll
+    parts = fields - 2
+    for p in range(parts):
+        lax.fori_loop(p * steps // parts, (p + 1) * steps // parts, solid, 0)
+        loads[5 + p].wait()
+        stores[2 + p].start()
     for j in range(back):
         solid_ref[j] = calm_ref[j] + pull_ref[j // 3] * solid_ref[j]
-    for f in range(2, fields):
-        loads[3 + f].wait()
-        stores[f].start()
     stores[fields].start()
     for store in stores:
         store.wait()

time: 48.2 us -> 48.4 us (level)
  no operation moved by 1% of the time
where the time goes in v8:
time: 48.4 us; the launch traced here: 48.3 us
  Pallas kernels  47.6 us (98%)
  between operations  0.64 us (1%)
    pallas_call x1, Pallas kernels, per_device(): pl.pallas_call(functools.partial(grid_kernel, n_gx, n_gy), out_shape=(sha...  43.4 us
    pallas_call x1, Pallas kernels, per_device(): pl.pallas_call(functools.partial(final_kernel, cap), out_shape=(shape((5,...  4.19 us

profile of v8, /device:TPU:0, one launch (start us, length us, event | category | flops | bytes accessed | tf_op | source)
XLA Modules:
  0.0 48.3 jit_solution(18097273926238814748)
XLA Ops:
  0.6 43.4 %advance_and_couple.1 = (f32[5,1536,128]{2,1,0:T(8,128)}, f32[32,32,128]{2,1,0:T(8,128)}, f32[4,128,128]{2,1,0:T(8,128)}, f32[2,128,128]{2,1,0:T(8,128)}) custom-call(f32[16,96,128]{2,1,0:T(8,128)} %rho_hbm.1, f32[3,16,96,128]{3,2,1,0:T(8,128)} %vel_hbm.1, f32[16,96,128]{2,1,0:T(8,128)} %temp_hbm.1, s32[1,256]{1,0:T(1,128)} %map_hbm.1, s32[1,64]{1,0:T(1,128)} %bitcast.4, ...), custom_call_target="tpu_custom_call" | custom-call | tf_op jit(solution)/shard_map/advance_and_couple/pallas_call | solution.py:615
  44.1 4.2 %place_results.1 = (f32[5,1536,128]{2,1,0:T(8,128)}, f32[4,128,128]{2,1,0:T(8,128)}) custom-call(s32[64]{0:T(128)} %rank_ref.1, f32[5,1536,128]{2,1,0:T(8,128)} %get-tuple-element.8.adv_ref, f32[32,32,128]{2,1,0:T(8,128)} %get-tuple-element.9.ret_hbm, f32[4,128,128]{2,1,0:T(8,128)} %get-tuple-element.10.calm_hbm, f32[2,128,128]{2,1,0:T(8,128)} %get-tuple-element.11.pull_hbm), custom_call_target="tpu_custom_call" | custom-call | tf_op jit(solution)/shard_map/place_results/pallas_call | solution.py:688
